TPU v7x, 32 devices: a whole 2x2x4 slice. The times are simulated.
32 devices in a mesh: tensor: 4 (over y, x), dp: 8 (over z, core).
Axes of the slice: x: 2, y: 2, z: 4, core: 2. Of those that a mesh axis runs over, the one named last changes fastest.
Arguments:
- inputs: float32 [3072, 1024], P('dp'), may hold values from -6 to 6
- cotangent: float32 [3072, 1024], P('dp'), may hold values from -6 to 6
- norm_gains: float32 [2, 1024], replicated, may hold values from 0.5 to 1.5
- mix_weight: float32 [1024, 8, 768], P('dp', 'tensor'), may hold values from -0.1875 to 0.1875
- gate_weight: float32 [1024, 2, 8], P('dp', None, 'tensor'), may hold values from -0.1875 to 0.1875
- conv_weight: float32 [4, 8, 512], P(None, 'tensor'), may hold values from -3 to 3
- a_log: float32 [8], P('tensor'), may hold values from -4 to 1
- dt_bias: float32 [8], P('tensor'), may hold values from -4 to -1
- out_gain: float32 [256], replicated, may hold values from 0.5 to 1.5
- out_weight: float32 [8, 256, 1024], P('tensor', None, 'dp'), may hold values from -0.25 to 0.25
- upgate_weight: float32 [1024, 2, 2816], P('dp', None, 'tensor'), may hold values from -0.1875 to 0.1875
- down_weight: float32 [2816, 1024], P('tensor', 'dp'), may hold values from -0.21875 to 0.21875
- moment_norm_gains: float32 [2, 1024], replicated, may hold values from -4 to 4
- moment_mix_weight: float32 [1024, 8, 768], P('dp', 'tensor'), may hold values from -4 to 4
- moment_gate_weight: float32 [1024, 2, 8], P('dp', None, 'tensor'), may hold values from -4 to 4
- moment_conv_weight: float32 [4, 8, 512], P(None, 'tensor'), may hold values from -4 to 4
- moment_a_log: float32 [8], P('tensor'), may hold values from -4 to 4
- moment_dt_bias: float32 [8], P('tensor'), may hold values from -4 to 4
- moment_out_gain: float32 [256], replicated, may hold values from -4 to 4
- moment_out_weight: float32 [8, 256, 1024], P('tensor', None, 'dp'), may hold values from -4 to 4
- moment_upgate_weight: float32 [1024, 2, 2816], P('dp', None, 'tensor'), may hold values from -4 to 4
- moment_down_weight: float32 [2816, 1024], P('tensor', 'dp'), may hold values from -4 to 4
- second_norm_gains: float32 [2, 1024], replicated, may hold values from 0.005 to 0.02
- second_mix_weight: float32 [1024, 8, 768], P('dp', 'tensor'), may hold values from 0.005 to 0.02
- second_gate_weight: float32 [1024, 2, 8], P('dp', None, 'tensor'), may hold values from 0.005 to 0.02
- second_conv_weight: float32 [4, 8, 512], P(None, 'tensor'), may hold values from 0.005 to 0.02
- second_a_log: float32 [8], P('tensor'), may hold values from 0.005 to 0.02
- second_dt_bias: float32 [8], P('tensor'), may hold values from 0.005 to 0.02
- second_out_gain: float32 [256], replicated, may hold values from 0.005 to 0.02
- second_out_weight: float32 [8, 256, 1024], P('tensor', None, 'dp'), may hold values from 0.005 to 0.02
- second_upgate_weight: float32 [1024, 2, 2816], P('dp', None, 'tensor'), may hold values from 0.005 to 0.02
- second_down_weight: float32 [2816, 1024], P('tensor', 'dp'), may hold values from 0.005 to 0.02
Outputs:
- outputs: float32 [3072, 1024], P('dp')
- grad_inputs: float32 [3072, 1024], P('dp')
- grad_norm_gains: float32 [2, 1024], replicated
- grad_mix_weight: float32 [1024, 8, 768], P('dp', 'tensor')
- grad_gate_weight: float32 [1024, 2, 8], P('dp', None, 'tensor')
- grad_conv_weight: float32 [4, 8, 512], P(None, 'tensor')
- grad_a_log: float32 [8], P('tensor')
- grad_dt_bias: float32 [8], P('tensor')
- grad_out_gain: float32 [256], replicated
- grad_out_weight: float32 [8, 256, 1024], P('tensor', None, 'dp')
- grad_upgate_weight: float32 [1024, 2, 2816], P('dp', None, 'tensor')
- grad_down_weight: float32 [2816, 1024], P('tensor', 'dp')
- new_norm_gains: float32 [2, 1024], replicated
- new_mix_weight: float32 [1024, 8, 768], P('dp', 'tensor')
- new_gate_weight: float32 [1024, 2, 8], P('dp', None, 'tensor')
- new_conv_weight: float32 [4, 8, 512], P(None, 'tensor')
- new_a_log: float32 [8], P('tensor')
- new_dt_bias: float32 [8], P('tensor')
- new_out_gain: float32 [256], replicated
- new_out_weight: float32 [8, 256, 1024], P('tensor', None, 'dp')
- new_upgate_weight: float32 [1024, 2, 2816], P('dp', None, 'tensor')
- new_down_weight: float32 [2816, 1024], P('tensor', 'dp')
- new_moment_norm_gains: float32 [2, 1024], replicated
- new_moment_mix_weight: float32 [1024, 8, 768], P('dp', 'tensor')
- new_moment_gate_weight: float32 [1024, 2, 8], P('dp', None, 'tensor')
- new_moment_conv_weight: float32 [4, 8, 512], P(None, 'tensor')
- new_moment_a_log: float32 [8], P('tensor')
- new_moment_dt_bias: float32 [8], P('tensor')
- new_moment_out_gain: float32 [256], replicated
- new_moment_out_weight: float32 [8, 256, 1024], P('tensor', None, 'dp')
- new_moment_upgate_weight: float32 [1024, 2, 2816], P('dp', None, 'tensor')
- new_moment_down_weight: float32 [2816, 1024], P('tensor', 'dp')
- new_second_norm_gains: float32 [2, 1024], replicated
- new_second_mix_weight: float32 [1024, 8, 768], P('dp', 'tensor')
- new_second_gate_weight: float32 [1024, 2, 8], P('dp', None, 'tensor')
- new_second_conv_weight: float32 [4, 8, 512], P(None, 'tensor')
- new_second_a_log: float32 [8], P('tensor')
- new_second_dt_bias: float32 [8], P('tensor')
- new_second_out_gain: float32 [256], replicated
- new_second_out_weight: float32 [8, 256, 1024], P('tensor', None, 'dp')
- new_second_upgate_weight: float32 [1024, 2, 2816], P('dp', None, 'tensor')
- new_second_down_weight: float32 [2816, 1024], P('tensor', 'dp')
All inputs are finite; a program needn't handle non-finite values.
Results may differ from a plain program's by a relative error of at most 0.02.
Values may be sent and summed in bfloat16 or wider, within the bound.
A program may use at most 192 MiB of HBM per device.

v0:
```python
import math

import jax
import jax.numpy as jnp
from jax import lax
from jax.sharding import PartitionSpec as P

DK = 128
DV = 256
CONV = 4
SPAN = 64
LEN = 384
STEP = 3


HIGHEST = lax.Precision.HIGHEST
RATE_MATRIX = 0.01
RATE_VECTOR = 0.1
CLIP_SHARE = 0.3


def rms_scale(rows_in, gain_row, epsilon):
    return (
        rows_in
        * lax.rsqrt(jnp.mean(rows_in * rows_in, axis=-1, keepdims=True) + epsilon)
        * gain_row
    )


def norm_apply(rows_in, gain_row):
    return rms_scale(rows_in, gain_row, 1e-05)


def unit_rows(rows_in):
    return rows_in * lax.rsqrt(jnp.sum(rows_in * rows_in, axis=-1, keepdims=True) + 1e-06)


def swiglu(paired):
    return jax.nn.silu(paired[:, 0]) * paired[:, 1]


def inverse_unit_lower(lower_part):
    size_now = lower_part.shape[-1]
    identity = jnp.eye(size_now, dtype=jnp.float32)
    inverse = identity - lower_part
    power_now = jnp.matmul(lower_part, lower_part, precision=HIGHEST)
    for repeat in range(size_now.bit_length() - 2):
        inverse = jnp.matmul(inverse, identity + power_now, precision=HIGHEST)
        power_now = jnp.matmul(power_now, power_now, precision=HIGHEST)
    return inverse


def delta_rule(queries, keys_now, values_now, beta_gate, decays):
    seq_count, length, head_count, key_size = keys_now.shape
    value_size = values_now.shape[-1]
    block_count = length // SPAN

    def to_blocks(array_in):
        shaped = array_in.reshape((seq_count, block_count, SPAN, head_count) + array_in.shape[3:])
        return jnp.moveaxis(shaped, (1, 3), (0, 2))

    strict = jnp.tril(jnp.ones((SPAN, SPAN), bool), -1)
    inclusive = jnp.tril(jnp.ones((SPAN, SPAN), bool))

    def block_step(state, block_items):
        query_block, key_block, value_block, beta_block, decay_block = block_items
        cumulative = jnp.cumsum(decay_block, axis=-1)
        log_gaps = cumulative[..., :, None] - cumulative[..., None, :]
        fall_strict = jnp.where(strict, jnp.exp(jnp.where(strict, log_gaps, 0.0)), 0.0)
        fall_inclusive = jnp.where(inclusive, jnp.exp(jnp.where(inclusive, log_gaps, 0.0)), 0.0)
        keys_keys = jnp.einsum("shtk,shuk->shtu", key_block, key_block, precision=HIGHEST)
        lower_part = beta_block[..., :, None] * keys_keys * fall_strict
        inverse = inverse_unit_lower(lower_part)
        growth = jnp.exp(cumulative)
        carried = jnp.einsum("shtk,shkv->shtv", key_block, state, precision=HIGHEST)
        right_side = beta_block[..., None] * (value_block - growth[..., None] * carried)
        new_values = jnp.einsum("shtu,shuv->shtv", inverse, right_side, precision=HIGHEST)
        scores = (
            jnp.einsum("shtk,shuk->shtu", query_block, key_block, precision=HIGHEST)
            * fall_inclusive
        )
        block_out = growth[..., None] * jnp.einsum(
            "shtk,shkv->shtv", query_block, state, precision=HIGHEST
        )
        block_out = block_out + jnp.einsum("shtu,shuv->shtv", scores, new_values, precision=HIGHEST)
        last_log = cumulative[..., -1:]
        tail_decay = jnp.exp(last_log - cumulative)
        state = jnp.exp(last_log)[..., None] * state + jnp.einsum(
            "shtk,shtv->shkv", key_block * tail_decay[..., None], new_values, precision=HIGHEST
        )
        return (state, block_out)

    zero_state = jnp.zeros((seq_count, head_count, key_size, value_size), jnp.float32)
    final_state, block_outs = lax.scan(
        block_step,
        zero_state,
        (
            to_blocks(queries),
            to_blocks(keys_now),
            to_blocks(values_now),
            to_blocks(beta_gate),
            to_blocks(decays),
        ),
    )
    block_outs = jnp.moveaxis(block_outs, (0, 2), (1, 3))
    return block_outs.reshape(seq_count, length, head_count, value_size)


def mixer_core(mixed_in, gate_in, conv_weight, a_log, dt_bias, out_gain):
    length = mixed_in.shape[1]
    key_size = DK
    qkv_width = 2 * DK + DV
    qkv_in = mixed_in[..., :qkv_width]
    padded = jnp.pad(qkv_in, ((0, 0), (CONV - 1, 0), (0, 0), (0, 0)))
    convolved = padded[:, 0:length] * conv_weight[0]
    for offset in range(1, CONV):
        convolved = convolved + padded[:, offset : offset + length] * conv_weight[offset]
    activated = jax.nn.silu(convolved)
    queries = unit_rows(activated[..., :key_size]) * key_size ** (-0.5)
    keys_now = unit_rows(activated[..., key_size : 2 * key_size])
    values_now = activated[..., 2 * key_size :]
    beta_gate = jax.nn.sigmoid(gate_in[:, :, 1])
    decays = -jnp.exp(a_log) * jax.nn.softplus(gate_in[:, :, 0] + dt_bias)
    core_raw = delta_rule(queries, keys_now, values_now, beta_gate, decays)
    return rms_scale(core_raw, out_gain, 1e-05) * jax.nn.silu(mixed_in[..., qkv_width:])


def adamw_update(weight, gradient, moment, second, rate, squares, entries):
    limit = CLIP_SHARE * math.sqrt(entries)
    scale = jnp.minimum(1.0, limit * lax.rsqrt(squares + 1e-12))
    clipped = gradient * scale
    new_moment = 0.9 * moment + 0.1 * clipped
    new_second = 0.95 * second + 0.05 * clipped * clipped
    first_fix = 1.0 - 0.9**STEP
    second_fix = 1.0 - 0.95**STEP
    update = new_moment / first_fix / (jnp.sqrt(new_second / second_fix) + 1e-08) + 0.1 * weight
    return (weight - rate * update, new_moment, new_second)


def square_sum(values):
    return jnp.sum(values * values)


def tensor_total(partial_value):
    return lax.psum(partial_value, "tensor")


def body(
    inputs,
    cotangent,
    norm_gains,
    mix_weight,
    gate_weight,
    conv_weight,
    a_log,
    dt_bias,
    out_gain,
    out_weight,
    upgate_weight,
    down_weight,
    moment_norm_gains,
    moment_mix_weight,
    moment_gate_weight,
    moment_conv_weight,
    moment_a_log,
    moment_dt_bias,
    moment_out_gain,
    moment_out_weight,
    moment_upgate_weight,
    moment_down_weight,
    second_norm_gains,
    second_mix_weight,
    second_gate_weight,
    second_conv_weight,
    second_a_log,
    second_dt_bias,
    second_out_gain,
    second_out_weight,
    second_upgate_weight,
    second_down_weight,
):
    mix_full, gate_full, out_full, upgate_full, down_full = (
        lax.all_gather(mix_weight.astype(jnp.bfloat16), "dp", axis=0, tiled=True),
        lax.all_gather(gate_weight.astype(jnp.bfloat16), "dp", axis=0, tiled=True),
        lax.all_gather(out_weight.astype(jnp.bfloat16), "dp", axis=2, tiled=True),
        lax.all_gather(upgate_weight.astype(jnp.bfloat16), "dp", axis=0, tiled=True),
        lax.all_gather(down_weight.astype(jnp.bfloat16), "dp", axis=1, tiled=True),
    )
    row_count, model_width = inputs.shape
    seq_count = row_count // LEN
    head_count = mix_full.shape[1]
    hidden_count = upgate_full.shape[2]
    normed_one = norm_apply(inputs, norm_gains[0]).astype(jnp.bfloat16)
    mixed_in = jnp.dot(
        normed_one, mix_full.reshape(model_width, -1), preferred_element_type=jnp.float32
    ).reshape(seq_count, LEN, head_count, -1)
    gate_in = jnp.dot(
        normed_one, gate_full.reshape(model_width, -1), preferred_element_type=jnp.float32
    ).reshape(seq_count, LEN, 2, head_count)
    core_out, core_back = jax.vjp(
        mixer_core, mixed_in, gate_in, conv_weight, a_log, dt_bias, out_gain
    )
    core_half = core_out.reshape(row_count, -1).astype(jnp.bfloat16)
    flat_out = out_full.reshape(-1, model_width)
    middle = inputs + tensor_total(jnp.dot(core_half, flat_out, preferred_element_type=jnp.float32))
    normed_rows = norm_apply(middle, norm_gains[1]).astype(jnp.bfloat16)
    flat_upgate = upgate_full.reshape(model_width, -1)
    paired = jnp.dot(normed_rows, flat_upgate, preferred_element_type=jnp.float32).reshape(
        row_count, 2, hidden_count
    )
    hidden_act, swiglu_back = jax.vjp(swiglu, paired)
    hidden_half = hidden_act.astype(jnp.bfloat16)
    output_rows = middle + tensor_total(
        jnp.dot(hidden_half, down_full, preferred_element_type=jnp.float32)
    )
    cot_half = cotangent.astype(jnp.bfloat16)
    grad_down = jnp.dot(hidden_half.T, cot_half, preferred_element_type=jnp.float32)
    grad_hidden = jnp.dot(cot_half, down_full.T, preferred_element_type=jnp.float32)
    grad_paired = swiglu_back(grad_hidden)[0].reshape(row_count, -1).astype(jnp.bfloat16)
    grad_upgate = jnp.dot(normed_rows.T, grad_paired, preferred_element_type=jnp.float32).reshape(
        upgate_full.shape
    )
    grad_normed_two = tensor_total(
        jnp.dot(grad_paired, flat_upgate.T, preferred_element_type=jnp.float32)
    )
    norm_two_back = jax.vjp(norm_apply, middle, norm_gains[1])[1]
    grad_from_second, grad_gain_two = norm_two_back(grad_normed_two)
    grad_middle = cotangent + grad_from_second
    middle_rows = grad_middle.astype(jnp.bfloat16)
    grad_out = jnp.dot(core_half.T, middle_rows, preferred_element_type=jnp.float32).reshape(
        out_full.shape
    )
    grad_core = jnp.dot(middle_rows, flat_out.T, preferred_element_type=jnp.float32).reshape(
        core_out.shape
    )
    grad_mixed, grad_gate_in, grad_conv, grad_a_log_part, grad_dt_part, grad_gain_part = core_back(
        grad_core
    )
    mixed_grad_half = grad_mixed.reshape(row_count, -1).astype(jnp.bfloat16)
    gate_grad_half = grad_gate_in.reshape(row_count, -1).astype(jnp.bfloat16)
    grad_mix = jnp.dot(normed_one.T, mixed_grad_half, preferred_element_type=jnp.float32).reshape(
        mix_full.shape
    )
    grad_gate = jnp.dot(normed_one.T, gate_grad_half, preferred_element_type=jnp.float32).reshape(
        gate_full.shape
    )
    partial_first = jnp.dot(
        mixed_grad_half, mix_full.reshape(model_width, -1).T, preferred_element_type=jnp.float32
    )
    partial_first = partial_first + jnp.dot(
        gate_grad_half, gate_full.reshape(model_width, -1).T, preferred_element_type=jnp.float32
    )
    grad_normed_one, gain_tensor_total = (
        lax.psum(partial_first.astype(jnp.bfloat16), "tensor").astype(jnp.float32),
        lax.psum(grad_gain_part.astype(jnp.bfloat16), "tensor").astype(jnp.float32),
    )
    norm_one_back = jax.vjp(norm_apply, inputs, norm_gains[0])[1]
    grad_from_first, grad_gain_one = norm_one_back(grad_normed_one)
    grad_input_rows = grad_middle + grad_from_first
    shard_mix, shard_gate, shard_out, shard_upgate, shard_down = (
        lax.psum_scatter(
            grad_mix.astype(jnp.bfloat16), "dp", scatter_dimension=0, tiled=True
        ).astype(jnp.float32),
        lax.psum_scatter(
            grad_gate.astype(jnp.bfloat16), "dp", scatter_dimension=0, tiled=True
        ).astype(jnp.float32),
        lax.psum_scatter(
            grad_out.astype(jnp.bfloat16), "dp", scatter_dimension=2, tiled=True
        ).astype(jnp.float32),
        lax.psum_scatter(
            grad_upgate.astype(jnp.bfloat16), "dp", scatter_dimension=0, tiled=True
        ).astype(jnp.float32),
        lax.psum_scatter(
            grad_down.astype(jnp.bfloat16), "dp", scatter_dimension=1, tiled=True
        ).astype(jnp.float32),
    )
    grad_norm_gains, grad_conv_weight, grad_a_log, grad_dt_bias, grad_out_gain = lax.psum(
        (
            jnp.stack([grad_gain_one, grad_gain_two]),
            grad_conv,
            grad_a_log_part,
            grad_dt_part,
            gain_tensor_total,
        ),
        "dp",
    )
    dp_count = lax.axis_size("dp")
    tensor_count = lax.axis_size("tensor")
    local_squares = jnp.stack(
        [
            square_sum(shard_mix),
            square_sum(shard_gate),
            square_sum(shard_out),
            square_sum(shard_upgate),
            square_sum(shard_down),
            square_sum(grad_conv_weight) / dp_count,
            square_sum(grad_a_log) / dp_count,
            square_sum(grad_dt_bias) / dp_count,
        ]
    )
    total_squares = lax.psum(local_squares, ("tensor", "dp"))
    spread = dp_count * tensor_count
    new_norm_gains, new_moment_norm_gains, new_second_norm_gains = adamw_update(
        norm_gains,
        grad_norm_gains,
        moment_norm_gains,
        second_norm_gains,
        RATE_VECTOR,
        square_sum(grad_norm_gains),
        grad_norm_gains.size,
    )
    new_mix_weight, new_moment_mix_weight, new_second_mix_weight = adamw_update(
        mix_weight,
        shard_mix,
        moment_mix_weight,
        second_mix_weight,
        RATE_MATRIX,
        total_squares[0],
        shard_mix.size * spread,
    )
    new_gate_weight, new_moment_gate_weight, new_second_gate_weight = adamw_update(
        gate_weight,
        shard_gate,
        moment_gate_weight,
        second_gate_weight,
        RATE_MATRIX,
        total_squares[1],
        shard_gate.size * spread,
    )
    new_conv_weight, new_moment_conv_weight, new_second_conv_weight = adamw_update(
        conv_weight,
        grad_conv_weight,
        moment_conv_weight,
        second_conv_weight,
        RATE_VECTOR,
        total_squares[5],
        grad_conv_weight.size * tensor_count,
    )
    new_a_log, new_moment_a_log, new_second_a_log = adamw_update(
        a_log,
        grad_a_log,
        moment_a_log,
        second_a_log,
        RATE_VECTOR,
        total_squares[6],
        grad_a_log.size * tensor_count,
    )
    new_dt_bias, new_moment_dt_bias, new_second_dt_bias = adamw_update(
        dt_bias,
        grad_dt_bias,
        moment_dt_bias,
        second_dt_bias,
        RATE_VECTOR,
        total_squares[7],
        grad_dt_bias.size * tensor_count,
    )
    new_out_gain, new_moment_out_gain, new_second_out_gain = adamw_update(
        out_gain,
        grad_out_gain,
        moment_out_gain,
        second_out_gain,
        RATE_VECTOR,
        square_sum(grad_out_gain),
        grad_out_gain.size,
    )
    new_out_weight, new_moment_out_weight, new_second_out_weight = adamw_update(
        out_weight,
        shard_out,
        moment_out_weight,
        second_out_weight,
        RATE_MATRIX,
        total_squares[2],
        shard_out.size * spread,
    )
    new_upgate_weight, new_moment_upgate_weight, new_second_upgate_weight = adamw_update(
        upgate_weight,
        shard_upgate,
        moment_upgate_weight,
        second_upgate_weight,
        RATE_MATRIX,
        total_squares[3],
        shard_upgate.size * spread,
    )
    new_down_weight, new_moment_down_weight, new_second_down_weight = adamw_update(
        down_weight,
        shard_down,
        moment_down_weight,
        second_down_weight,
        RATE_MATRIX,
        total_squares[4],
        shard_down.size * spread,
    )
    return (
        output_rows,
        grad_input_rows,
        grad_norm_gains,
        shard_mix,
        shard_gate,
        grad_conv_weight,
        grad_a_log,
        grad_dt_bias,
        grad_out_gain,
        shard_out,
        shard_upgate,
        shard_down,
        new_norm_gains,
        new_mix_weight,
        new_gate_weight,
        new_conv_weight,
        new_a_log,
        new_dt_bias,
        new_out_gain,
        new_out_weight,
        new_upgate_weight,
        new_down_weight,
        new_moment_norm_gains,
        new_moment_mix_weight,
        new_moment_gate_weight,
        new_moment_conv_weight,
        new_moment_a_log,
        new_moment_dt_bias,
        new_moment_out_gain,
        new_moment_out_weight,
        new_moment_upgate_weight,
        new_moment_down_weight,
        new_second_norm_gains,
        new_second_mix_weight,
        new_second_gate_weight,
        new_second_conv_weight,
        new_second_a_log,
        new_second_dt_bias,
        new_second_out_gain,
        new_second_out_weight,
        new_second_upgate_weight,
        new_second_down_weight,
    )


def solution(mesh):
    placed = (
        P("dp", None),
        P("dp", None),
        P(),
        P("dp", "tensor", None),
        P("dp", None, "tensor"),
        P(None, "tensor", None),
        P("tensor"),
        P("tensor"),
        P(),
        P("tensor", None, "dp"),
        P("dp", None, "tensor"),
        P("tensor", "dp"),
        P(),
        P("dp", "tensor", None),
        P("dp", None, "tensor"),
        P(None, "tensor", None),
        P("tensor"),
        P("tensor"),
        P(),
        P("tensor", None, "dp"),
        P("dp", None, "tensor"),
        P("tensor", "dp"),
        P(),
        P("dp", "tensor", None),
        P("dp", None, "tensor"),
        P(None, "tensor", None),
        P("tensor"),
        P("tensor"),
        P(),
        P("tensor", None, "dp"),
        P("dp", None, "tensor"),
        P("tensor", "dp"),
    )
    return jax.shard_map(
        body,
        mesh=mesh,
        in_specs=placed,
        out_specs=(
            P("dp", None),
            P("dp", None),
            P(),
            P("dp", "tensor", None),
            P("dp", None, "tensor"),
            P(None, "tensor", None),
            P("tensor"),
            P("tensor"),
            P(),
            P("tensor", None, "dp"),
            P("dp", None, "tensor"),
            P("tensor", "dp"),
            P(),
            P("dp", "tensor", None),
            P("dp", None, "tensor"),
            P(None, "tensor", None),
            P("tensor"),
            P("tensor"),
            P(),
            P("tensor", None, "dp"),
            P("dp", None, "tensor"),
            P("tensor", "dp"),
            P(),
            P("dp", "tensor", None),
            P("dp", None, "tensor"),
            P(None, "tensor", None),
            P("tensor"),
            P("tensor"),
            P(),
            P("tensor", None, "dp"),
            P("dp", None, "tensor"),
            P("tensor", "dp"),
            P(),
            P("dp", "tensor", None),
            P("dp", None, "tensor"),
            P(None, "tensor", None),
            P("tensor"),
            P("tensor"),
            P(),
            P("tensor", None, "dp"),
            P("dp", None, "tensor"),
            P("tensor", "dp"),
        ),
        check_vma=False,
    )
```

profile of v0, /device:TPU:0, one launch (start us, length us, event | category | flops | bytes accessed | tf_op | source)
XLA Modules:
  0.0 1074.3 jit_solution(3819606815029483734)
XLA Ops:
  12.2 13.5 %all_gather.15 = bf16[1024,2,2]{0,2,1:T(2,128)(2,1)S(1)} all-gather(bf16[128,2,2]{0,2,1:T(2,128)(2,1)S(1)} %convert_element_type.123), channel_id=1, replica_groups=mesh['tensor'=4,'dp'=8] {'dp'}, dimensions={0}, use_global_device_ids=true | all-gather | bytes 9216 | tf_op jit(solution)/shard_map/all_gather | solution.py:184
  28.5 22.8 %all-gather.5.cloned.1.call-done = bf16[1024,2,768]{2,1,0:T(2,128)(2,1)} async-done(((bf16[128,2,768]{2,1,0:T(2,128)(2,1)}), bf16[1024,2,768]{2,1,0:T(2,128)(2,1)}) %all-gather.5.cloned.1.call-update) | async-done | bytes 3145744 | tf_op jit(solution)/shard_map/all_gather | solution.py:183
  51.3 4.1 copy.325
  55.5 4.7 copy.195
  60.2 3.3 convolution_bitcast_fusion.10
  76.2 154.1 %while.128 = (s32[]{:T(128)}, f32[1,2,128,256]{3,2,1,0:T(8,128)S(1)}, f32[6,1,2,64,256]{4,3,2,1,0:T(8,128)S(1)}, f32[6,1,2,64,64]{4,3,2,1,0:T(8,128)}, f32[6,1,2...) while((s32[]{:T(128)}, ...), condition=%wide.region_5.6_spmd.clone.clone, body=%wide.region_3.5_spmd.clone.clone.sunk | while | flops 290373888 | bytes 7649046 | solution.py:94
  234.2 3.1 fusion.344
  240.4 56.9 %all-reduce.25.cloned.1.call-done = f32[384,1024]{1,0:T(8,128)} async-done(((f32[384,1024]{1,0:T(8,128)}), f32[384,1024]{1,0:T(8,128)}) %all-reduce.25.cloned.1.call-update) | async-done | bytes 1572880 | tf_op jit(solution)/shard_map/psum | solution.py:145
  300.0 36.4 %all-gather.9.cloned.1.call-done = bf16[1024,2,704]{0,2,1:T(8,128)(2,1)} async-done(((bf16[128,2,704]{0,2,1:T(8,128)(2,1)}), bf16[1024,2,704]{0,2,1:T(8,128)(2,1)}) %all-gather.9.cloned.1.call-update) | async-done | bytes 2883600 | tf_op jit(solution)/shard_map/all_gather | solution.py:186
  336.4 5.4 fusion.263
  341.8 21.5 %all-gather.11.cloned.1.call-done = bf16[704,1024]{1,0:T(8,128)(2,1)} async-done(((bf16[704,128]{1,0:T(8,128)(2,1)}), bf16[704,1024]{1,0:T(8,128)(2,1)}) %all-gather.11.cloned.1.call-update) | async-done | bytes 1441808 | tf_op jit(solution)/shard_map/all_gather | solution.py:187
  363.3 3.8 multiply_bitcast_fusion
  373.2 3.6 convolution_convert_fusion.2
  376.8 3.0 copy.256
  379.8 79.6 %all-reduce.29.cloned.1.call-done = (f32[384,1024]{1,0:T(8,128)}, f32[384,1024]{1,0:T(8,128)}) async-done(((f32[384,1024]{1,0:T(8,128)}, f32[384,1024]{1,0:T(8,128)}), (f32[384,1024]{1,0:T(8,128)}, f32[384,1024]{1,0:T(8,128)})) %all-reduce.29.cloned.1.call-update) | async-done | bytes 3145744 | tf_op jit(solution)/shard_map/psum | solution.py:145
  459.4 3.0 multiply_reduce_fusion.5
  462.4 3.6 fusion.269
  470.0 3.5 multiply_reduce_fusion.10
  477.7 299.4 %while.129 = (s32[]{:T(128)}, f32[1,2,128,256]{2,3,1,0:T(8,128)S(1)}, f32[6,1,2,64,128]{4,3,2,1,0:T(8,128)}, f32[6,1,2,64,128]{4,3,2,1,0:T(8,128)}, f32[6,1,2,64...) while((s32[]{:T(128)}, ...), condition=%wide.region_24.25_spmd.clone.clone, body=%wide.region_13.24_spmd.clone.clone.sunk | while | flops 580387328 | bytes 18202404 | solution.py:94
  790.8 3.2 multiply_reduce_fusion.3
  801.0 4.8 fusion.346
  810.6 3.6 copy.252
  816.8 5.4 convolution_convert_fusion.1
  822.2 4.6 copy.260
  826.8 5.0 convolution_convert_fusion
  834.5 8.9 psum.85
  845.7 41.5 %all-reduce.27.cloned.1.call-done = bf16[384,1024]{1,0:T(8,128)(2,1)} async-done(((bf16[384,1024]{1,0:T(8,128)(2,1)}), bf16[384,1024]{1,0:T(8,128)(2,1)}) %all-reduce.27.cloned.1.call-update) | async-done | bytes 786448 | tf_op jit(solution)/shard_map/psum | solution.py:254
  888.9 28.8 %all-reduce.19 = (f32[2,1024]{1,0:T(2,128)S(1)}, f32[4,2,512]{2,1,0:T(2,128)S(1)}, f32[2]{0:T(128)S(1)}, f32[2]{0:T(128)S(1)}, f32[256]{0:T(256)S(1)}) all-reduce(f32[2,1024]{1,0:T(2,128)S(1)} %pad_maximum_fusion, f32[4,2,512]{2,1,0:T(2,128)S(1)} %pad_add_fusion.3, ...), channel_id=1, replica_groups=mesh['tensor'=4,'dp'=8] {'dp'}, use_global_device_ids=true, to_apply=%region_31.32 | all-reduce | flops 6404 | bytes 50720 | tf_op jit(solution)/shard_map/psum | solution.py:277
  929.6 31.7 %reduce-scatter.20.cloned.1.call-done = bf16[128,1408]{1,0:T(8,128)(2,1)} async-done(((bf16[1024,1408]{1,0:T(8,128)(2,1)}), bf16[128,1408]{1,0:T(8,128)(2,1)}) %reduce-scatter.20.cloned.1.call-update) | async-done | bytes 360464
  963.3 39.8 %reduce-scatter.14.cloned.1.call-done = bf16[128,2,768]{2,0,1:T(8,128)(2,1)} async-done(((bf16[1024,2,768]{2,0,1:T(8,128)(2,1)}), bf16[128,2,768]{2,0,1:T(8,128)(2,1)}) %reduce-scatter.14.cloned.1.call-update) | async-done | bytes 393232 | tf_op jit(solution)/shard_map/reduce_scatter | solution.py:261
  1004.9 3.3 stack.41
  1008.8 38.0 %psum.87 = f32[8]{0:T(128)S(1)} all-reduce(f32[8]{0:T(128)S(1)} %stack.41), channel_id=1, replica_groups=mesh['tensor'=4,'dp'=8] {'tensor','dp'}, use_global_device_ids=true, to_apply=%region_58.59 | all-reduce | flops 8 | bytes 64 | tf_op jit(solution)/shard_map/psum | solution.py:301
  (1022 shorter events, 556.8 us)
Async XLA Ops:
  7.3 44.1 %all-gather.5.cloned.1.call-start = ((), (), s32[]{:S(2)}) async-start(), calls=%async_computation.5 | async-start | bytes 3538944 | tf_op jit(solution)/shard_map/all_gather | solution.py:183
  9.6 224.6 %all-gather.7.cloned.1.call-start = ((), (), s32[]{:S(2)}) async-start(), calls=%async_computation.6 | async-start | bytes 1179648 | tf_op jit(solution)/shard_map/all_gather | solution.py:185
  10.4 286.9 %all-reduce.25.cloned.1.call-start = ((), (), s32[]{:S(2)}) async-start(), calls=%async_computation.7 | async-start | bytes 3145728 | tf_op jit(solution)/shard_map/psum | solution.py:145
  12.1 52.9 %copy-start.66 = (f32[2,512]{1,0:T(2,128)}, f32[2,512]{1,0:T(2,128)S(1)}, u32[]{:S(2)}) copy-start(f32[2,512]{1,0:T(2,128)S(1)} %get-tuple-element.3339) | copy-start | bytes 12292
  12.2 52.8 %copy-start.68 = (f32[2,512]{1,0:T(2,128)}, f32[2,512]{1,0:T(2,128)S(1)}, u32[]{:S(2)}) copy-start(f32[2,512]{1,0:T(2,128)S(1)} %get-tuple-element.3340) | copy-start | bytes 12292
  237.3 99.1 %all-gather.9.cloned.1.call-start = ((), (), s32[]{:S(2)}) async-start(), calls=%async_computation.8 | async-start | bytes 3244032 | tf_op jit(solution)/shard_map/all_gather | solution.py:186
  239.3 124.0 %all-gather.11.cloned.1.call-start = ((), (), s32[]{:S(2)}) async-start(), calls=%async_computation.9 | async-start | bytes 1622016 | tf_op jit(solution)/shard_map/all_gather | solution.py:187
  240.1 96.3 %copy-start.61 = (f32[1,1024]{1,0:T(1,128)S(1)}, f32[1,1024]{1,0:T(1,128)}, u32[]{:S(2)}) copy-start(f32[1,1024]{1,0:T(1,128)} %get-tuple-element.3343) | copy-start | bytes 12292
  240.1 219.3 %all-reduce.29.cloned.1.call-start = ((), (), s32[]{:S(2)}) async-start(), calls=%async_computation.16 | async-start | bytes 6291456 | tf_op jit(solution)/shard_map/psum | solution.py:145
  300.0 162.4 %copy-start.79 = (f32[384]{0:T(512)}, f32[384]{0:T(512)S(1)}, u32[]{:S(2)}) copy-start(f32[384]{0:T(512)S(1)} %fusion.321) | copy-start | bytes 4612
  373.1 458.9 %reduce-scatter.22.cloned.1.call-start = ((), (), s32[]{:S(2)}) async-start(), calls=%async_computation.15 | async-start | bytes 1769472
  379.8 464.0 %reduce-scatter.16.cloned.1.call-start = ((), (), s32[]{:S(2)}) async-start(), calls=%async_computation.12 | async-start | bytes 294912
  805.9 81.3 %all-reduce.27.cloned.1.call-start = ((), (), s32[]{:S(2)}) async-start(), calls=%async_computation.10 | async-start | bytes 1572864 | tf_op jit(solution)/shard_map/psum | solution.py:254
  808.9 118.8 %reduce-scatter.18.cloned.1.call-start = ((), (), s32[]{:S(2)}) async-start(), calls=%async_computation.13 | async-start | bytes 1179648
  816.7 144.5 %reduce-scatter.20.cloned.1.call-start = ((), (), s32[]{:S(2)}) async-start(), calls=%async_computation.14 | async-start | bytes 3244032
  826.8 176.3 %reduce-scatter.14.cloned.1.call-start = ((), (), s32[]{:S(2)}) async-start(), calls=%async_computation.11 | async-start | bytes 3538944 | tf_op jit(solution)/shard_map/reduce_scatter | solution.py:261
  831.9 55.4 %copy-start.60 = (f32[1,1024]{1,0:T(1,128)S(1)}, f32[1,1024]{1,0:T(1,128)}, u32[]{:S(2)}) copy-start(f32[1,1024]{1,0:T(1,128)} %copy-done.59) | copy-start | bytes 12292
  831.9 55.4 %copy-start.78 = (f32[384]{0:T(512)S(1)}, f32[384]{0:T(512)}, u32[]{:S(2)}) copy-start(f32[384]{0:T(512)} %copy-done.77) | copy-start | bytes 4612
  833.1 55.8 %copy-start.94 = (f32[1024]{0:T(1024)S(1)}, f32[1024]{0:T(1024)}, u32[]{:S(2)}) copy-start(f32[1024]{0:T(1024)} %get-tuple-element.3005) | copy-start | bytes 12292
  833.1 91.1 %copy-start.90 = (f32[384]{0:T(512)S(1)}, f32[384]{0:T(512)}, u32[]{:S(2)}) copy-start(f32[384]{0:T(512)} %copy-done.89) | copy-start | bytes 4612
  833.1 91.1 %copy-start.75 = (f32[2,1024]{1,0:T(2,128)S(1)}, f32[2,1024]{1,0:T(2,128)}, u32[]{:S(2)}) copy-start(f32[2,1024]{1,0:T(2,128)} %param.38) | copy-start | bytes 24580
  833.1 91.1 %copy-start.101 = (f32[2,1024]{1,0:T(2,128)S(1)}, f32[2,1024]{1,0:T(2,128)}, u32[]{:S(2)}) copy-start(f32[2,1024]{1,0:T(2,128)} %param.48) | copy-start | bytes 24580
  833.1 91.1 %copy-start.102 = (f32[2,1024]{1,0:T(2,128)S(1)}, f32[2,1024]{1,0:T(2,128)}, u32[]{:S(2)}) copy-start(f32[2,1024]{1,0:T(2,128)} %param.58) | copy-start | bytes 24580
  917.8 142.8 %copy-start.58 = (f32[4,2,512]{2,1,0:T(2,128)}, f32[4,2,512]{2,1,0:T(2,128)S(1)}, u32[]{:S(2)}) copy-start(f32[4,2,512]{2,1,0:T(2,128)S(1)} %get-tuple-element.3213) | copy-start | bytes 49156
  927.6 80.6 %copy-start.93 = (f32[256]{0:T(256)S(1)}, f32[256]{0:T(256)}, u32[]{:S(2)}) copy-start(f32[256]{0:T(256)} %param.44) | copy-start | bytes 3076
  927.6 80.6 %copy-start.113 = (f32[256]{0:T(256)S(1)}, f32[256]{0:T(256)}, u32[]{:S(2)}) copy-start(f32[256]{0:T(256)} %param.54) | copy-start | bytes 3076
  927.6 80.6 %copy-start.114 = (f32[256]{0:T(256)S(1)}, f32[256]{0:T(256)}, u32[]{:S(2)}) copy-start(f32[256]{0:T(256)} %param.64) | copy-start | bytes 3076
  927.6 80.6 %copy-start.116 = (f32[256]{0:T(256)S(1)}, f32[256]{0:T(256)}, u32[]{:S(2)}) copy-start(f32[256]{0:T(256)} %copy-done.115) | copy-start | bytes 3076
  927.6 125.3 %copy-start.27 = (f32[128,2,768]{2,1,0:T(2,128)S(1)}, f32[128,2,768]{2,1,0:T(2,128)}, u32[]{:S(2)}) copy-start(f32[128,2,768]{2,1,0:T(2,128)} %param.39) | copy-start | bytes 2359300
  927.6 125.3 %copy-start.37 = (f32[128,2,768]{2,1,0:T(2,128)S(1)}, f32[128,2,768]{2,1,0:T(2,128)}, u32[]{:S(2)}) copy-start(f32[128,2,768]{2,1,0:T(2,128)} %param.49) | copy-start | bytes 2359300
  929.6 134.6 %copy-start.36 = (f32[2,256,128]{2,1,0:T(8,128)}, f32[2,256,128]{2,1,0:T(8,128)S(1)}, u32[]{:S(2)}) copy-start(f32[2,256,128]{2,1,0:T(8,128)S(1)} %get-tuple-element.3253) | copy-start | bytes 786436
  963.3 99.2 %copy-start.30 = (f32[128,2,704]{0,2,1:T(8,128)}, f32[128,2,704]{0,2,1:T(8,128)S(1)}, u32[]{:S(2)}) copy-start(f32[128,2,704]{0,2,1:T(8,128)S(1)} %get-tuple-element.3251) | copy-start | bytes 2162692
  (150 other events, 1079.9 us)
Sparse Core Ops, SparseCore 0:
  10.3 40.9 all-gather.4
  53.5 22.8 all-gather.6
  237.4 59.7 all-reduce.24
  299.4 37.0 all-gather.8
  338.5 24.7 all-gather.10
  373.2 86.0 all-reduce.28
  461.7 34.2 reduce-scatter.21
  806.0 30.3 reduce-scatter.15
  840.3 46.9 all-reduce.26
  889.4 32.2 reduce-scatter.17
  924.0 37.1 reduce-scatter.19
  963.4 39.5 reduce-scatter.13
where the time goes:
time: 1100 us; the launch traced here: 1070 us
  matrix products  400 us (36%)
  waiting for transfers between devices  330 us (30%)
  local copies, waits for them, and re-layouts  117 us (11%)
  other arithmetic  109 us (10%)
  blocking collectives  89.3 us (8%)
  between operations  25 us (2%)
    psum x2, waiting for transfers between devices, tensor_total(): return lax.psum(partial_value, 'tensor')  136 us
    dot_general x90, matrix products, inverse_unit_lower(): inverse = jnp.matmul(inverse, identity + power_now, precision=HIGHEST)  97.6 us
    dot_general x72, matrix products, inverse_unit_lower(): power_now = jnp.matmul(power_now, power_now, precision=HIGHEST)  73.3 us
    psum x1, waiting for transfers between devices, body(): lax.psum(partial_first.astype(jnp.bfloat16), 'tensor').astype(jnp.float32)  41.5 us
    reduce_scatter x1, waiting for transfers between devices, body(): lax.psum_scatter(grad_mix.astype(jnp.bfloat16), 'dp', scatter_dimension=0...  39.8 us
    psum x1, blocking collectives, body(): total_squares = lax.psum(local_squares, ('tensor', 'dp'))  38 us
    all_gather x1, waiting for transfers between devices, body(): lax.all_gather(upgate_weight.astype(jnp.bfloat16), 'dp', axis=0, tiled=True)  36.4 us
    unnamed x260, local copies, waits for them, and re-layouts  34.7 us
  transfers between devices with their start and end apart: 12, of which 8 were waited for; matrix products, arithmetic and copies ran while one was open for 55% of the time, Pallas kernels for 0%

commit v1 on v0

--- a/solution.py
+++ b/solution.py
@@ -39,88 +39,144 @@
     return jax.nn.silu(paired[:, 0]) * paired[:, 1]
 
 
-def inverse_unit_lower(lower_part):
+HIGH = lax.Precision.HIGH
+
+
+def unit_lower_product(lower_part):
     size_now = lower_part.shape[-1]
     identity = jnp.eye(size_now, dtype=jnp.float32)
     inverse = identity - lower_part
     power_now = jnp.matmul(lower_part, lower_part, precision=HIGHEST)
-    for repeat in range(size_now.bit_length() - 2):
-        inverse = jnp.matmul(inverse, identity + power_now, precision=HIGHEST)
-        power_now = jnp.matmul(power_now, power_now, precision=HIGHEST)
+    steps = size_now.bit_length() - 2
+    for repeat in range(steps):
+        inverse = inverse + jnp.matmul(inverse, power_now, precision=HIGHEST)
+        if repeat + 1 < steps:
+            power_now = jnp.matmul(power_now, power_now, precision=HIGHEST)
     return inverse
 
 
+@jax.custom_vjp
+def inverse_unit_lower(lower_part):
+    return unit_lower_product(lower_part)
+
+
+def inverse_forward(lower_part):
+    inverse = unit_lower_product(lower_part)
+    return inverse, inverse
+
+
+def inverse_backward(inverse, grad_inverse):
+    flipped = jnp.swapaxes(inverse, -1, -2)
+    inner = jnp.matmul(flipped, grad_inverse, precision=HIGH)
+    return (-jnp.matmul(inner, flipped, precision=HIGH),)
+
+
+inverse_unit_lower.defvjp(inverse_forward, inverse_backward)
+
+
+def run_states(steps_in, adds_in):
+    block_count = steps_in.shape[2]
+    state = jnp.zeros_like(adds_in[:, :, 0])
+    states = [state]
+    for index in range(block_count - 1):
+        state = adds_in[:, :, index] + jnp.matmul(steps_in[:, :, index], state, precision=HIGH)
+        states.append(state)
+    return jnp.stack(states, axis=2)
+
+
+@jax.custom_vjp
+def chain_states(steps_in, adds_in):
+    return run_states(steps_in, adds_in)
+
+
+def chain_forward(steps_in, adds_in):
+    states = run_states(steps_in, adds_in)
+    return states, (steps_in, states)
+
+
+def chain_backward(kept, grad_states):
+    steps_in, states = kept
+    block_count = steps_in.shape[2]
+    grad_now = jnp.zeros_like(grad_states[:, :, 0])
+    grads = [grad_now]
+    for index in range(block_count - 1, 0, -1):
+        if index == block_count - 1:
+            grad_now = grad_states[:, :, index]
+        else:
+            grad_now = grad_states[:, :, index] + jnp.einsum(
+                "shkj,shkv->shjv", steps_in[:, :, index], grad_now, precision=HIGH
+            )
+        grads.append(grad_now)
+    grad_adds = jnp.stack(grads[::-1], axis=2)
+    grad_steps = jnp.einsum("shnkv,shnjv->shnkj", grad_adds, states, precision=HIGH)
+    return grad_steps, grad_adds
+
+
+chain_states.defvjp(chain_forward, chain_backward)
+
+
 def delta_rule(queries, keys_now, values_now, beta_gate, decays):
-    seq_count, length, head_count, key_size = keys_now.shape
-    value_size = values_now.shape[-1]
+    seq_count, head_count, length, key_size = keys_now.shape
     block_count = length // SPAN
 
     def to_blocks(array_in):
-        shaped = array_in.reshape((seq_count, block_count, SPAN, head_count) + array_in.shape[3:])
-        return jnp.moveaxis(shaped, (1, 3), (0, 2))
+        return array_in.reshape((seq_count, head_count, block_count, SPAN) + array_in.shape[3:])
 
     strict = jnp.tril(jnp.ones((SPAN, SPAN), bool), -1)
     inclusive = jnp.tril(jnp.ones((SPAN, SPAN), bool))
-
-    def block_step(state, block_items):
-        query_block, key_block, value_block, beta_block, decay_block = block_items
-        cumulative = jnp.cumsum(decay_block, axis=-1)
-        log_gaps = cumulative[..., :, None] - cumulative[..., None, :]
-        fall_strict = jnp.where(strict, jnp.exp(jnp.where(strict, log_gaps, 0.0)), 0.0)
-        fall_inclusive = jnp.where(inclusive, jnp.exp(jnp.where(inclusive, log_gaps, 0.0)), 0.0)
-        keys_keys = jnp.einsum("shtk,shuk->shtu", key_block, key_block, precision=HIGHEST)
-        lower_part = beta_block[..., :, None] * keys_keys * fall_strict
-        inverse = inverse_unit_lower(lower_part)
-        growth = jnp.exp(cumulative)
-        carried = jnp.einsum("shtk,shkv->shtv", key_block, state, precision=HIGHEST)
-        right_side = beta_block[..., None] * (value_block - growth[..., None] * carried)
-        new_values = jnp.einsum("shtu,shuv->shtv", inverse, right_side, precision=HIGHEST)
-        scores = (
-            jnp.einsum("shtk,shuk->shtu", query_block, key_block, precision=HIGHEST)
-            * fall_inclusive
-        )
-        block_out = growth[..., None] * jnp.einsum(
-            "shtk,shkv->shtv", query_block, state, precision=HIGHEST
-        )
-        block_out = block_out + jnp.einsum("shtu,shuv->shtv", scores, new_values, precision=HIGHEST)
-        last_log = cumulative[..., -1:]
-        tail_decay = jnp.exp(last_log - cumulative)
-        state = jnp.exp(last_log)[..., None] * state + jnp.einsum(
-            "shtk,shtv->shkv", key_block * tail_decay[..., None], new_values, precision=HIGHEST
-        )
-        return (state, block_out)
-
-    zero_state = jnp.zeros((seq_count, head_count, key_size, value_size), jnp.float32)
-    final_state, block_outs = lax.scan(
-        block_step,
-        zero_state,
-        (
-            to_blocks(queries),
-            to_blocks(keys_now),
-            to_blocks(values_now),
-            to_blocks(beta_gate),
-            to_blocks(decays),
-        ),
-    )
-    block_outs = jnp.moveaxis(block_outs, (0, 2), (1, 3))
-    return block_outs.reshape(seq_count, length, head_count, value_size)
+    queries, keys_now, values_now, beta_gate, decays = (
+        to_blocks(queries),
+        to_blocks(keys_now),
+        to_blocks(values_now),
+        to_blocks(beta_gate),
+        to_blocks(decays),
+    )
+    cumulative = jnp.einsum(
+        "shnu,tu->shnt", decays, inclusive.astype(jnp.float32), precision=HIGHEST
+    )
+    log_gaps = cumulative[..., :, None] - cumulative[..., None, :]
+    fall_inclusive = jnp.where(inclusive, jnp.exp(jnp.where(inclusive, log_gaps, 0.0)), 0.0)
+    fall_strict = jnp.where(strict, fall_inclusive, 0.0)
+    both = jnp.concatenate([keys_now, queries], axis=3)
+    products = jnp.einsum("shntk,shnuk->shntu", both, keys_now, precision=HIGH)
+    lower_part = beta_gate[..., None] * products[..., :SPAN, :] * fall_strict
+    scores = products[..., SPAN:, :] * fall_inclusive
+    inverse = inverse_unit_lower(lower_part)
+    growth = jnp.exp(cumulative)
+    sides = jnp.concatenate(
+        [(beta_gate * growth)[..., None] * keys_now, beta_gate[..., None] * values_now], axis=-1
+    )
+    solved = jnp.einsum("shntu,shnuw->shntw", inverse, sides, precision=HIGH)
+    last_log = cumulative[..., -1:]
+    tail_keys = keys_now * jnp.exp(last_log - cumulative)[..., None]
+    joined = jnp.einsum("shntk,shntw->shnkw", tail_keys, solved, precision=HIGH)
+    identity = jnp.eye(key_size, dtype=jnp.float32)
+    steps_in = jnp.exp(last_log)[..., None] * identity - joined[..., :key_size]
+    states = chain_states(steps_in, joined[..., key_size:])
+    readers = jnp.concatenate([solved[..., :key_size], growth[..., None] * queries], axis=3)
+    read = jnp.einsum("shntk,shnkv->shntv", readers, states, precision=HIGH)
+    new_values = solved[..., key_size:] - read[..., :SPAN, :]
+    block_outs = read[..., SPAN:, :] + jnp.einsum(
+        "shntu,shnuv->shntv", scores, new_values, precision=HIGH
+    )
+    return block_outs.reshape(values_now.shape[:2] + (length, values_now.shape[-1]))
 
 
 def mixer_core(mixed_in, gate_in, conv_weight, a_log, dt_bias, out_gain):
-    length = mixed_in.shape[1]
+    length = mixed_in.shape[2]
     key_size = DK
     qkv_width = 2 * DK + DV
     qkv_in = mixed_in[..., :qkv_width]
-    padded = jnp.pad(qkv_in, ((0, 0), (CONV - 1, 0), (0, 0), (0, 0)))
-    convolved = padded[:, 0:length] * conv_weight[0]
+    padded = jnp.pad(qkv_in, ((0, 0), (0, 0), (CONV - 1, 0), (0, 0)))
+    convolved = padded[:, :, 0:length] * conv_weight[0][:, None]
     for offset in range(1, CONV):
-        convolved = convolved + padded[:, offset : offset + length] * conv_weight[offset]
+        convolved = convolved + padded[:, :, offset : offset + length] * conv_weight[offset][:, None]
     activated = jax.nn.silu(convolved)
     queries = unit_rows(activated[..., :key_size]) * key_size ** (-0.5)
     keys_now = unit_rows(activated[..., key_size : 2 * key_size])
     values_now = activated[..., 2 * key_size :]
-    beta_gate = jax.nn.sigmoid(gate_in[:, :, 1])
-    decays = -jnp.exp(a_log) * jax.nn.softplus(gate_in[:, :, 0] + dt_bias)
+    beta_gate = jax.nn.sigmoid(gate_in[:, 1])
+    decays = -jnp.exp(a_log)[:, None] * jax.nn.softplus(gate_in[:, 0] + dt_bias[:, None])
     core_raw = delta_rule(queries, keys_now, values_now, beta_gate, decays)
     return rms_scale(core_raw, out_gain, 1e-05) * jax.nn.silu(mixed_in[..., qkv_width:])
 
@@ -139,6 +195,13 @@
 
 def square_sum(values):
     return jnp.sum(values * values)
+
+
+def gathered_total(flat_value, axis_names):
+    columns = -(-flat_value.size // 1024) * 128
+    block = jnp.pad(flat_value, (0, 8 * columns - flat_value.size)).reshape(8, columns)
+    blocks = lax.all_gather(block, axis_names, axis=0, tiled=True)
+    return jnp.sum(blocks.reshape(-1, 8, columns), axis=0).reshape(-1)
 
 
 def tensor_total(partial_value):
@@ -179,30 +242,53 @@
     second_upgate_weight,
     second_down_weight,
 ):
-    mix_full, gate_full, out_full, upgate_full, down_full = (
-        lax.all_gather(mix_weight.astype(jnp.bfloat16), "dp", axis=0, tiled=True),
-        lax.all_gather(gate_weight.astype(jnp.bfloat16), "dp", axis=0, tiled=True),
-        lax.all_gather(out_weight.astype(jnp.bfloat16), "dp", axis=2, tiled=True),
-        lax.all_gather(upgate_weight.astype(jnp.bfloat16), "dp", axis=0, tiled=True),
-        lax.all_gather(down_weight.astype(jnp.bfloat16), "dp", axis=1, tiled=True),
-    )
+    owned_rows = mix_weight.shape[0]
+    head_count = mix_weight.shape[1]
+    hidden_count = upgate_weight.shape[2]
+    mix_columns = mix_weight.size // owned_rows
+    gate_columns = gate_weight.size // owned_rows
+    joint_shard = jnp.concatenate(
+        [
+            mix_weight.astype(jnp.bfloat16).reshape(owned_rows, -1),
+            gate_weight.astype(jnp.bfloat16).reshape(owned_rows, -1),
+            jnp.zeros((owned_rows, 128 - gate_columns), jnp.bfloat16),
+        ],
+        axis=1,
+    )
+    joint_full = lax.all_gather(joint_shard, "dp", axis=0, tiled=True)
+    out_full = lax.all_gather(out_weight.astype(jnp.bfloat16), "dp", axis=2, tiled=True)
+    upgate_full = lax.all_gather(
+        upgate_weight.astype(jnp.bfloat16), "dp", axis=0, tiled=True
+    )
+    down_full = lax.all_gather(down_weight.astype(jnp.bfloat16), "dp", axis=1, tiled=True)
     row_count, model_width = inputs.shape
     seq_count = row_count // LEN
-    head_count = mix_full.shape[1]
-    hidden_count = upgate_full.shape[2]
     normed_one = norm_apply(inputs, norm_gains[0]).astype(jnp.bfloat16)
-    mixed_in = jnp.dot(
-        normed_one, mix_full.reshape(model_width, -1), preferred_element_type=jnp.float32
-    ).reshape(seq_count, LEN, head_count, -1)
-    gate_in = jnp.dot(
-        normed_one, gate_full.reshape(model_width, -1), preferred_element_type=jnp.float32
-    ).reshape(seq_count, LEN, 2, head_count)
+    joint_in = jnp.dot(normed_one, joint_full, preferred_element_type=jnp.float32)
+    mixed_in = jnp.swapaxes(
+        joint_in[:, :mix_columns].reshape(seq_count, LEN, head_count, -1), 1, 2
+    )
+    gate_in = jnp.moveaxis(
+        joint_in[:, mix_columns : mix_columns + gate_columns].reshape(
+            seq_count, LEN, 2, head_count
+        ),
+        1,
+        3,
+    )
     core_out, core_back = jax.vjp(
         mixer_core, mixed_in, gate_in, conv_weight, a_log, dt_bias, out_gain
     )
-    core_half = core_out.reshape(row_count, -1).astype(jnp.bfloat16)
+    core_half = (
+        jnp.swapaxes(core_out.astype(jnp.bfloat16), 1, 2).reshape(row_count, -1)
+    )
     flat_out = out_full.reshape(-1, model_width)
-    middle = inputs + tensor_total(jnp.dot(core_half, flat_out, preferred_element_type=jnp.float32))
+    middle_part = jnp.dot(core_half, flat_out, preferred_element_type=jnp.float32).astype(
+        jnp.bfloat16
+    )
+    middle_part, upgate_full, down_full = lax.optimization_barrier(
+        (middle_part, upgate_full, down_full)
+    )
+    middle = inputs + tensor_total(middle_part).astype(jnp.float32)
     normed_rows = norm_apply(middle, norm_gains[1]).astype(jnp.bfloat16)
     flat_upgate = upgate_full.reshape(model_width, -1)
     paired = jnp.dot(normed_rows, flat_upgate, preferred_element_type=jnp.float32).reshape(
@@ -210,19 +296,32 @@
     )
     hidden_act, swiglu_back = jax.vjp(swiglu, paired)
     hidden_half = hidden_act.astype(jnp.bfloat16)
-    output_rows = middle + tensor_total(
-        jnp.dot(hidden_half, down_full, preferred_element_type=jnp.float32)
-    )
     cot_half = cotangent.astype(jnp.bfloat16)
-    grad_down = jnp.dot(hidden_half.T, cot_half, preferred_element_type=jnp.float32)
     grad_hidden = jnp.dot(cot_half, down_full.T, preferred_element_type=jnp.float32)
     grad_paired = swiglu_back(grad_hidden)[0].reshape(row_count, -1).astype(jnp.bfloat16)
-    grad_upgate = jnp.dot(normed_rows.T, grad_paired, preferred_element_type=jnp.float32).reshape(
-        upgate_full.shape
-    )
     grad_normed_two = tensor_total(
-        jnp.dot(grad_paired, flat_upgate.T, preferred_element_type=jnp.float32)
-    )
+        jnp.dot(grad_paired, flat_upgate.T, preferred_element_type=jnp.float32).astype(
+            jnp.bfloat16
+        )
+    )
+    output_part = jnp.dot(hidden_half, down_full, preferred_element_type=jnp.float32).astype(
+        jnp.bfloat16
+    )
+    grad_down = jnp.dot(
+        hidden_half.T, cot_half, preferred_element_type=jnp.float32
+    ).astype(jnp.bfloat16)
+    grad_upgate = (
+        jnp.dot(normed_rows.T, grad_paired, preferred_element_type=jnp.float32)
+        .astype(jnp.bfloat16)
+        .reshape(upgate_full.shape)
+    )
+    grad_normed_two, output_part, grad_down, grad_upgate = lax.optimization_barrier(
+        (grad_normed_two, output_part, grad_down, grad_upgate)
+    )
+    grad_normed_two = grad_normed_two.astype(jnp.float32)
+    shard_upgate = lax.psum_scatter(grad_upgate, "dp", scatter_dimension=0, tiled=True)
+    shard_down = lax.psum_scatter(grad_down, "dp", scatter_dimension=1, tiled=True)
+    output_total = tensor_total(output_part)
     norm_two_back = jax.vjp(norm_apply, middle, norm_gains[1])[1]
     grad_from_second, grad_gain_two = norm_two_back(grad_normed_two)
     grad_middle = cotangent + grad_from_second
@@ -230,62 +329,67 @@
     grad_out = jnp.dot(core_half.T, middle_rows, preferred_element_type=jnp.float32).reshape(
         out_full.shape
     )
-    grad_core = jnp.dot(middle_rows, flat_out.T, preferred_element_type=jnp.float32).reshape(
-        core_out.shape
+    shard_out = lax.psum_scatter(
+        grad_out.astype(jnp.bfloat16), "dp", scatter_dimension=2, tiled=True
+    )
+    grad_core = jnp.swapaxes(
+        jnp.dot(middle_rows, flat_out.T, preferred_element_type=jnp.float32).reshape(
+            seq_count, LEN, head_count, -1
+        ),
+        1,
+        2,
     )
     grad_mixed, grad_gate_in, grad_conv, grad_a_log_part, grad_dt_part, grad_gain_part = core_back(
         grad_core
     )
-    mixed_grad_half = grad_mixed.reshape(row_count, -1).astype(jnp.bfloat16)
-    gate_grad_half = grad_gate_in.reshape(row_count, -1).astype(jnp.bfloat16)
-    grad_mix = jnp.dot(normed_one.T, mixed_grad_half, preferred_element_type=jnp.float32).reshape(
-        mix_full.shape
-    )
-    grad_gate = jnp.dot(normed_one.T, gate_grad_half, preferred_element_type=jnp.float32).reshape(
-        gate_full.shape
+    joint_grad_half = jnp.concatenate(
+        [
+            jnp.swapaxes(grad_mixed.astype(jnp.bfloat16), 1, 2).reshape(row_count, -1),
+            jnp.moveaxis(grad_gate_in.astype(jnp.bfloat16), 3, 1).reshape(row_count, -1),
+            jnp.zeros((row_count, 128 - gate_columns), jnp.bfloat16),
+        ],
+        axis=1,
     )
     partial_first = jnp.dot(
-        mixed_grad_half, mix_full.reshape(model_width, -1).T, preferred_element_type=jnp.float32
-    )
-    partial_first = partial_first + jnp.dot(
-        gate_grad_half, gate_full.reshape(model_width, -1).T, preferred_element_type=jnp.float32
-    )
-    grad_normed_one, gain_tensor_total = (
-        lax.psum(partial_first.astype(jnp.bfloat16), "tensor").astype(jnp.float32),
-        lax.psum(grad_gain_part.astype(jnp.bfloat16), "tensor").astype(jnp.float32),
+        joint_grad_half, joint_full.T, preferred_element_type=jnp.float32
+    ).astype(jnp.bfloat16)
+    partial_first, output_total, shard_upgate, shard_down, shard_out = lax.optimization_barrier(
+        (partial_first, output_total, shard_upgate, shard_down, shard_out)
+    )
+    output_rows = middle + output_total.astype(jnp.float32)
+    shard_upgate, shard_down, shard_out = (
+        shard_upgate.astype(jnp.float32),
+        shard_down.astype(jnp.float32),
+        shard_out.astype(jnp.float32),
+    )
+    grad_normed_one = lax.psum(partial_first, "tensor").astype(jnp.float32)
+    grad_joint = jnp.dot(normed_one.T, joint_grad_half, preferred_element_type=jnp.float32)
+    shard_joint = lax.psum_scatter(
+        grad_joint.astype(jnp.bfloat16), "dp", scatter_dimension=0, tiled=True
+    ).astype(jnp.float32)
+    shard_mix = shard_joint[:, :mix_columns].reshape(mix_weight.shape)
+    shard_gate = shard_joint[:, mix_columns : mix_columns + gate_columns].reshape(
+        gate_weight.shape
     )
     norm_one_back = jax.vjp(norm_apply, inputs, norm_gains[0])[1]
     grad_from_first, grad_gain_one = norm_one_back(grad_normed_one)
     grad_input_rows = grad_middle + grad_from_first
-    shard_mix, shard_gate, shard_out, shard_upgate, shard_down = (
-        lax.psum_scatter(
-            grad_mix.astype(jnp.bfloat16), "dp", scatter_dimension=0, tiled=True
-        ).astype(jnp.float32),
-        lax.psum_scatter(
-            grad_gate.astype(jnp.bfloat16), "dp", scatter_dimension=0, tiled=True
-        ).astype(jnp.float32),
-        lax.psum_scatter(
-            grad_out.astype(jnp.bfloat16), "dp", scatter_dimension=2, tiled=True
-        ).astype(jnp.float32),
-        lax.psum_scatter(
-            grad_upgate.astype(jnp.bfloat16), "dp", scatter_dimension=0, tiled=True
-        ).astype(jnp.float32),
-        lax.psum_scatter(
-            grad_down.astype(jnp.bfloat16), "dp", scatter_dimension=1, tiled=True
-        ).astype(jnp.float32),
-    )
-    grad_norm_gains, grad_conv_weight, grad_a_log, grad_dt_bias, grad_out_gain = lax.psum(
-        (
-            jnp.stack([grad_gain_one, grad_gain_two]),
-            grad_conv,
-            grad_a_log_part,
-            grad_dt_part,
-            gain_tensor_total,
-        ),
-        "dp",
-    )
     dp_count = lax.axis_size("dp")
     tensor_count = lax.axis_size("tensor")
+    early = jnp.concatenate(
+        [
+            grad_conv.reshape(-1),
+            grad_gain_two.reshape(-1),
+            grad_a_log_part.reshape(-1),
+            grad_dt_part.reshape(-1),
+        ]
+    )
+    early = gathered_total(early, "dp")
+    cut = [grad_conv.size, model_width, a_log.size, dt_bias.size]
+    grad_conv_weight = early[: cut[0]].reshape(conv_weight.shape)
+    grad_gain_two = early[cut[0] : cut[0] + cut[1]]
+    grad_a_log = early[cut[0] + cut[1] : cut[0] + cut[1] + cut[2]]
+    grad_dt_bias = early[cut[0] + cut[1] + cut[2] : sum(cut)]
     local_squares = jnp.stack(
         [
             square_sum(shard_mix),
@@ -298,7 +402,11 @@
             square_sum(grad_dt_bias) / dp_count,
         ]
     )
-    total_squares = lax.psum(local_squares, ("tensor", "dp"))
+    late = jnp.concatenate([grad_gain_one / tensor_count, grad_gain_part, local_squares])
+    late = gathered_total(late, ("tensor", "dp"))
+    grad_norm_gains = jnp.stack([late[:model_width], grad_gain_two])
+    grad_out_gain = late[model_width : model_width + out_gain.size]
+    total_squares = late[model_width + out_gain.size : model_width + out_gain.size + 8]
     spread = dp_count * tensor_count
     new_norm_gains, new_moment_norm_gains, new_second_norm_gains = adamw_update(
         norm_gains,

time: 1100 us -> 609 us (0.55); the launches traced: 1070 us -> 604 us
  matrix products: 400 us -> 77.9 us
  local copies, waits for them, and re-layouts: 117 us -> 63.8 us
  other arithmetic: 109 us -> 62.7 us
  blocking collectives: 89.3 us -> 54.3 us
  waiting for transfers between devices: 330 us -> 319 us
    dot_general x312 -> x42, matrix products: 371 us -> 50.1 us  [the longest x3 8.02 us: delta_rule(): joined = jnp.einsum('shntk,shntw->shnkw', tail_keys, solved, precision=HIGH)]
    psum x3 -> x0, blocking collectives: 75.7 us -> none  [the longest x1 38 us: body(): total_squares = lax.psum(local_squares, ('tensor', 'dp'))]
    all_gather x1 -> x2, blocking collectives: 13.5 us -> 54.3 us  [gathered_total(): blocks = lax.all_gather(block, axis_names, axis=0, tiled=True)]
    psum x1, waiting for transfers between devices: 41.5 us -> 21.2 us  [body(): grad_normed_one = lax.psum(partial_first, 'tensor').astype(jnp.float32)]
    reduce_sum x32 -> x7, other arithmetic: 22.8 us -> 4.14 us  [the longest x1 2.33 us: mixer_core(): padded[:, :, offset:offset + length] * conv_weight[offset][:, None]]
    dynamic_update_slice x30 -> x0, other arithmetic: 16.3 us -> none  [delta_rule(): lax.scan(block_step, zero_state, (to_blocks(queries), to_blocks(keys_now)...]
    all_gather x1, waiting for transfers between devices: 22.8 us -> 38.4 us  [body(): joint_full = lax.all_gather(joint_shard, 'dp', axis=0, tiled=True)]
    dynamic_slice x24 -> x0, local copies, waits for them, and re-layouts: 15 us -> none  [delta_rule(): lax.scan(block_step, zero_state, (to_blocks(queries), to_blocks(keys_now)...]
  transfers between devices with their start and end apart: 12 -> 12, of which waited for: 8 -> 9; matrix products, arithmetic and copies ran while one was open for 55% -> 23% of each run, Pallas kernels for 0% -> 0%
where the time goes in v1:
time: 609 us; the launch traced here: 604 us
  waiting for transfers between devices  319 us (52%)
  matrix products  77.9 us (13%)
  local copies, waits for them, and re-layouts  63.8 us (10%)
  other arithmetic  62.7 us (10%)
  blocking collectives  54.3 us (9%)
  between operations  25.6 us (4%)
    psum x3, waiting for transfers between devices, tensor_total(): return lax.psum(partial_value, 'tensor')  132 us
    all_gather x2, blocking collectives, gathered_total(): blocks = lax.all_gather(block, axis_names, axis=0, tiled=True)  54.3 us
    reduce_scatter x1, waiting for transfers between devices, body(): lax.psum_scatter(grad_joint.astype(jnp.bfloat16), 'dp', scatter_dimension...  41.5 us
    all_gather x1, waiting for transfers between devices, body(): joint_full = lax.all_gather(joint_shard, 'dp', axis=0, tiled=True)  38.4 us
    all_gather x1, waiting for transfers between devices, body(): lax.all_gather(upgate_weight.astype(jnp.bfloat16), 'dp', axis=0, tiled=True)  37.8 us
    unnamed x342, local copies, waits for them, and re-layouts  32.1 us
    unnamed x15, waiting for transfers between devices  30 us
    psum x1, waiting for transfers between devices, body(): grad_normed_one = lax.psum(partial_first, 'tensor').astype(jnp.float32)  21.2 us
  transfers between devices with their start and end apart: 12, of which 9 were waited for; matrix products, arithmetic and copies ran while one was open for 23% of the time, Pallas kernels for 0%

profile of v1, /device:TPU:0, one launch (start us, length us, event | category | flops | bytes accessed | tf_op | source)
XLA Modules:
  0.0 604.1 jit_solution(10163311980484338355)
XLA Ops:
  15.5 38.4 %all-gather.5.cloned.1.call-done = bf16[1024,1664]{1,0:T(8,128)(2,1)} async-done(((bf16[128,1664]{1,0:T(8,128)(2,1)}), bf16[1024,1664]{1,0:T(8,128)(2,1)}) %all-gather.5.cloned.1.call-update) | async-done | bytes 3407888 | tf_op jit(solution)/shard_map/all_gather | solution.py:258
  53.8 3.6 fusion.197
  57.9 2.8 reshape.1084
  86.2 2.8 convolution_convert_fusion.6
  89.1 17.8 %all-gather.11.cloned.1.call-done = bf16[704,1024]{1,0:T(8,128)(2,1)} async-done(((bf16[704,128]{1,0:T(8,128)(2,1)}), bf16[704,1024]{1,0:T(8,128)(2,1)}) %all-gather.11.cloned.1.call-update) | async-done | bytes 1441808 | tf_op jit(solution)/shard_map/all_gather | solution.py:263
  106.9 37.8 %all-gather.9.cloned.1.call-done = bf16[1024,2,704]{0,2,1:T(8,128)(2,1)} async-done(((bf16[128,2,704]{0,2,1:T(8,128)(2,1)}), bf16[1024,2,704]{0,2,1:T(8,128)(2,1)}) %all-gather.9.cloned.1.call-update) | async-done | bytes 2883600 | tf_op jit(solution)/shard_map/all_gather | solution.py:260
  144.7 50.4 %all-reduce.34.cloned.1.call-done = bf16[384,1024]{1,0:T(8,128)(2,1)} async-done(((bf16[384,1024]{1,0:T(8,128)(2,1)}), bf16[384,1024]{1,0:T(8,128)(2,1)}) %all-reduce.34.cloned.1.call-update) | async-done | bytes 786448 | tf_op jit(solution)/shard_map/psum | solution.py:208
  197.8 2.6 fusion
  206.2 4.7 convolution_convert_fusion
  210.9 5.2 copy.230
  216.0 3.2 convolution_convert_fusion.4
  219.3 3.6 convolution_convert_fusion.2
  222.9 32.1 %all-reduce.36.cloned.1.call-done = bf16[384,1024]{1,0:T(8,128)(2,1)} async-done(((bf16[384,1024]{1,0:T(8,128)(2,1)}), bf16[384,1024]{1,0:T(8,128)(2,1)}) %all-reduce.36.cloned.1.call-update) | async-done | bytes 786448 | tf_op jit(solution)/shard_map/psum | solution.py:208
  260.7 3.7 copy.276
  266.9 4.5 copy.278
  271.5 2.6 copy.274
  274.1 4.7 multiply_reduce_fusion.7
  283.2 2.9 fusion.39
  294.1 3.9 fusion.36
  324.9 3.3 pad_add_fusion
  329.8 5.2 concatenate.25
  336.1 4.5 convolution_convert_fusion.5
  343.6 29.7 %reduce-scatter.13.cloned.1.call-done = bf16[128,1408]{1,0:T(8,128)(2,1)} async-done(((bf16[1024,1408]{1,0:T(8,128)(2,1)}), bf16[128,1408]{1,0:T(8,128)(2,1)}) %reduce-scatter.13.cloned.1.call-update) | async-done | bytes 360464
  375.2 49.7 %all-reduce.38.cloned.1.call-done = bf16[384,1024]{1,0:T(8,128)(2,1)} async-done(((bf16[384,1024]{1,0:T(8,128)(2,1)}), bf16[384,1024]{1,0:T(8,128)(2,1)}) %all-reduce.38.cloned.1.call-update) | async-done | bytes 786448 | tf_op jit(solution)/shard_map/psum | solution.py:208
  425.0 5.2 convolution_convert_fusion.1
  431.4 14.2 %all_gather.22 = f32[64,768]{1,0:T(8,128)S(1)} all-gather(f32[8,768]{1,0:T(8,128)S(1)} %reshape.1120), channel_id=1, replica_groups=mesh['tensor'=4,'dp'=8] {'dp'}, dimensions={0}, use_global_device_ids=true | all-gather | bytes 221184 | tf_op jit(solution)/shard_map/all_gather | solution.py:203
  452.3 2.7 multiply_reduce_fusion.11
  456.4 21.2 %all-reduce.40.cloned.1.call-done = bf16[384,1024]{1,0:T(8,128)(2,1)} async-done(((bf16[384,1024]{1,0:T(8,128)(2,1)}), bf16[384,1024]{1,0:T(8,128)(2,1)}) %all-reduce.40.cloned.1.call-update) | async-done | bytes 786448 | tf_op jit(solution)/shard_map/psum | solution.py:365
  480.9 41.5 %reduce-scatter.11.cloned.1.call-done = bf16[128,1664]{1,0:T(8,128)(2,1)} async-done(((bf16[1024,1664]{1,0:T(8,128)(2,1)}), bf16[128,1664]{1,0:T(8,128)(2,1)}) %reduce-scatter.11.cloned.1.call-update) | async-done | bytes 426000 | tf_op jit(solution)/shard_map/reduce_scatter | solution.py:367
  524.9 3.3 concatenate.27
  528.3 40.1 %all_gather.23 = f32[256,256]{1,0:T(8,128)S(1)} all-gather(f32[8,256]{1,0:T(8,128)S(1)} %reshape.1123), channel_id=1, replica_groups=mesh['tensor'=4,'dp'=8] {'tensor','dp'}, dimensions={0}, use_global_device_ids=true | all-gather | bytes 270336 | tf_op jit(solution)/shard_map/all_gather | solution.py:203
  593.2 3.9 multiply_subtract_fusion
  (531 shorter events, 126.7 us)
Async XLA Ops:
  7.2 46.6 %all-gather.5.cloned.1.call-start = ((), (), s32[]{:S(2)}) async-start(), calls=%async_computation.4 | async-start | bytes 3833856 | tf_op jit(solution)/shard_map/all_gather | solution.py:258
  10.5 75.6 %all-gather.7.cloned.1.call-start = ((), (), s32[]{:S(2)}) async-start(), calls=%async_computation.5 | async-start | bytes 1179648 | tf_op jit(solution)/shard_map/all_gather | solution.py:259
  11.3 95.6 %all-gather.11.cloned.1.call-start = ((), (), s32[]{:S(2)}) async-start(), calls=%async_computation.7 | async-start | bytes 1622016 | tf_op jit(solution)/shard_map/all_gather | solution.py:263
  12.1 132.6 %all-gather.9.cloned.1.call-start = ((), (), s32[]{:S(2)}) async-start(), calls=%async_computation.6 | async-start | bytes 3244032 | tf_op jit(solution)/shard_map/all_gather | solution.py:260
  13.0 182.2 %all-reduce.34.cloned.1.call-start = ((), (), s32[]{:S(2)}) async-start(), calls=%async_computation.8 | async-start | bytes 1572864 | tf_op jit(solution)/shard_map/psum | solution.py:208
  14.4 48.3 %copy-start.156 = (f32[2]{0:T(128)}, f32[2]{0:T(128)S(1)}, u32[]{:S(2)}) copy-start(f32[2]{0:T(128)S(1)} %exponential_negate_fusion) | copy-start | bytes 28
  14.6 42.8 %copy-start.141 = (f32[384]{0:T(512)}, f32[384]{0:T(512)S(1)}, u32[]{:S(2)}) copy-start(f32[384]{0:T(512)S(1)} %multiply_reduce_fusion.5) | copy-start | bytes 4612
  14.6 42.8 %copy-start.139 = (f32[384]{0:T(512)}, f32[384]{0:T(512)S(1)}, u32[]{:S(2)}) copy-start(f32[384]{0:T(512)S(1)} %fusion.178) | copy-start | bytes 4612
  14.7 55.0 %copy-start.116 = (pred[64,64]{0,1:T(8,128)(4,1)}, pred[64,64]{0,1:T(8,128)(4,1)S(1)}, u32[]{:S(2)}) copy-start(pred[64,64]{0,1:T(8,128)(4,1)S(1)} %iota_compare_fusion.2) | copy-start | bytes 12292
  14.8 54.8 %copy-start.84 = (pred[64,64]{0,1:T(8,128)(4,1)}, pred[64,64]{0,1:T(8,128)(4,1)S(1)}, u32[]{:S(2)}) copy-start(pred[64,64]{0,1:T(8,128)(4,1)S(1)} %copy.209) | copy-start | bytes 12292
  15.4 42.0 %copy-start.111 = (f32[1,1024]{1,0:T(1,128)}, f32[1,1024]{1,0:T(1,128)S(1)}, u32[]{:S(2)}) copy-start(f32[1,1024]{1,0:T(1,128)S(1)} %get-tuple-element.212) | copy-start | bytes 12292
  15.4 48.9 %copy-start.103 = (f32[2,512]{1,0:T(2,128)}, f32[2,512]{1,0:T(2,128)S(1)}, u32[]{:S(2)}) copy-start(f32[2,512]{1,0:T(2,128)S(1)} %get-tuple-element.199) | copy-start | bytes 12292
  15.4 48.9 %copy-start.105 = (f32[2,512]{1,0:T(2,128)}, f32[2,512]{1,0:T(2,128)S(1)}, u32[]{:S(2)}) copy-start(f32[2,512]{1,0:T(2,128)S(1)} %get-tuple-element.200) | copy-start | bytes 12292
  15.4 48.9 %copy-start.107 = (f32[2,512]{1,0:T(2,128)}, f32[2,512]{1,0:T(2,128)S(1)}, u32[]{:S(2)}) copy-start(f32[2,512]{1,0:T(2,128)S(1)} %get-tuple-element.201) | copy-start | bytes 12292
  15.4 48.9 %copy-start.109 = (f32[2,512]{1,0:T(2,128)}, f32[2,512]{1,0:T(2,128)S(1)}, u32[]{:S(2)}) copy-start(f32[2,512]{1,0:T(2,128)S(1)} %get-tuple-element.202) | copy-start | bytes 12292
  86.2 58.6 %copy-start.60 = (bf16[1,384,2,256]{1,3,2,0:T(8,128)(2,1)}, bf16[1,384,2,256]{1,3,2,0:T(8,128)(2,1)S(1)}, u32[]{:S(2)}) copy-start(bf16[1,384,2,256]{1,3,2,0:T(8,128)(2,1)S(1)} %copy.229) | copy-start | bytes 1179652
  144.7 110.3 %all-reduce.36.cloned.1.call-start = ((), (), s32[]{:S(2)}) async-start(), calls=%async_computation.9 | async-start | bytes 1572864 | tf_op jit(solution)/shard_map/psum | solution.py:208
  206.1 134.5 %reduce-scatter.17.cloned.1.call-start = ((), (), s32[]{:S(2)}) async-start(), calls=%async_computation.15 | async-start | bytes 1179648
  266.9 74.9 %reduce-scatter.15.cloned.1.call-start = ((), (), s32[]{:S(2)}) async-start(), calls=%async_computation.14 | async-start | bytes 1769472
  283.1 90.2 %reduce-scatter.13.cloned.1.call-start = ((), (), s32[]{:S(2)}) async-start(), calls=%async_computation.13 | async-start | bytes 3244032
  293.9 131.0 %all-reduce.38.cloned.1.call-start = ((), (), s32[]{:S(2)}) async-start(), calls=%async_computation.10 | async-start | bytes 1572864 | tf_op jit(solution)/shard_map/psum | solution.py:208
  324.6 152.9 %all-reduce.40.cloned.1.call-start = ((), (), s32[]{:S(2)}) async-start(), calls=%async_computation.11 | async-start | bytes 1572864 | tf_op jit(solution)/shard_map/psum | solution.py:365
  340.6 84.4 %copy-start.1 = (f32[384,1024]{1,0:T(8,128)S(1)}, f32[384,1024]{1,0:T(8,128)}, u32[]{:S(2)}) copy-start(f32[384,1024]{1,0:T(8,128)} %param.32) | copy-start | bytes 4718596
  340.6 84.4 %copy-start.112 = (f32[1,1024]{1,0:T(1,128)S(1)}, f32[1,1024]{1,0:T(1,128)}, u32[]{:S(2)}) copy-start(f32[1,1024]{1,0:T(1,128)} %copy-done.111) | copy-start | bytes 12292
  340.6 84.4 %copy-start.140 = (f32[384]{0:T(512)S(1)}, f32[384]{0:T(512)}, u32[]{:S(2)}) copy-start(f32[384]{0:T(512)} %copy-done.139) | copy-start | bytes 4612
  424.9 97.4 %reduce-scatter.11.cloned.1.call-start = ((), (), s32[]{:S(2)}) async-start(), calls=%async_computation.12 | async-start | bytes 3833856 | tf_op jit(solution)/shard_map/reduce_scatter | solution.py:367
  446.2 139.4 %copy-start.99 = (f32[4,2,512]{2,1,0:T(2,128)}, f32[4,2,512]{2,1,0:T(2,128)S(1)}, u32[]{:S(2)}) copy-start(f32[4,2,512]{2,1,0:T(2,128)S(1)} %get-tuple-element.165) | copy-start | bytes 49156
  452.3 136.1 %copy-start.65 = (f32[704,128]{1,0:T(8,128)}, f32[704,128]{1,0:T(8,128)S(1)}, u32[]{:S(2)}) copy-start(f32[704,128]{1,0:T(8,128)S(1)} %get-tuple-element.167) | copy-start | bytes 1081348
  456.4 22.9 %copy-start.142 = (f32[384]{0:T(512)S(1)}, f32[384]{0:T(512)}, u32[]{:S(2)}) copy-start(f32[384]{0:T(512)} %copy-done.141) | copy-start | bytes 4612
  456.4 22.9 %copy-start.15 = (f32[384,1024]{1,0:T(8,128)S(1)}, f32[384,1024]{1,0:T(8,128)}, u32[]{:S(2)}) copy-start(f32[384,1024]{1,0:T(8,128)} %copy-done.14) | copy-start | bytes 4718596
  480.9 44.0 %copy-start.158 = (f32[256]{0:T(256)S(1)}, f32[256]{0:T(256)}, u32[]{:S(2)}) copy-start(f32[256]{0:T(256)} %get-tuple-element.108) | copy-start | bytes 3076
  522.4 46.6 %copy-start.38 = (bf16[128,1664]{1,0:T(8,128)(2,1)S(1)}, bf16[128,1664]{1,0:T(8,128)(2,1)}, u32[]{:S(2)}) copy-start(bf16[128,1664]{1,0:T(8,128)(2,1)} %reduce-scatter.11.cloned.1.call-done) | copy-start | bytes 1277956
  (144 other events, 554.6 us)
Sparse Core Ops, SparseCore 0:
  10.6 43.1 all-gather.4
  56.0 22.8 all-gather.6
  81.0 25.8 all-gather.10
  108.9 35.7 all-gather.8
  148.1 46.9 all-reduce.33
  206.2 48.7 all-reduce.35
  267.0 32.3 reduce-scatter.16
  301.7 32.2 reduce-scatter.14
  336.4 36.9 reduce-scatter.12
  376.8 48.0 all-reduce.37
  428.8 48.7 all-reduce.39
  479.8 42.5 reduce-scatter.10

commit v2 on v1

--- a/solution.py
+++ b/solution.py
@@ -204,8 +204,34 @@
     return jnp.sum(blocks.reshape(-1, 8, columns), axis=0).reshape(-1)
 
 
-def tensor_total(partial_value):
-    return lax.psum(partial_value, "tensor")
+def exchange_total(part, bits, half_width):
+    total = part
+    for bit in bits:
+        pairs = [(index, index ^ bit) for index in range(lax.axis_size("tensor"))]
+        if half_width:
+            rounded = lax.reduce_precision(total, 8, 7)
+            other = lax.ppermute(rounded.astype(jnp.bfloat16), "tensor", pairs)
+            total = rounded.astype(jnp.float32) + other.astype(jnp.float32)
+        else:
+            total = total + lax.ppermute(total, "tensor", pairs)
+    return total
+
+
+def tensor_total(partial_value, half_width=True):
+    tensor_count = lax.axis_size("tensor")
+    if tensor_count & (tensor_count - 1):
+        return lax.psum(partial_value, "tensor")
+    bits = [1 << place for place in range(tensor_count.bit_length() - 1)]
+    if not half_width:
+        return exchange_total(partial_value, bits, False)
+    middle_row = partial_value.shape[0] // 2
+    return jnp.concatenate(
+        [
+            exchange_total(partial_value[:middle_row], bits, True),
+            exchange_total(partial_value[middle_row:], bits[::-1], True),
+        ],
+        axis=0,
+    )
 
 
 def body(
@@ -282,13 +308,8 @@
         jnp.swapaxes(core_out.astype(jnp.bfloat16), 1, 2).reshape(row_count, -1)
     )
     flat_out = out_full.reshape(-1, model_width)
-    middle_part = jnp.dot(core_half, flat_out, preferred_element_type=jnp.float32).astype(
-        jnp.bfloat16
-    )
-    middle_part, upgate_full, down_full = lax.optimization_barrier(
-        (middle_part, upgate_full, down_full)
-    )
-    middle = inputs + tensor_total(middle_part).astype(jnp.float32)
+    middle_part = jnp.dot(core_half, flat_out, preferred_element_type=jnp.float32)
+    middle = inputs + tensor_total(middle_part)
     normed_rows = norm_apply(middle, norm_gains[1]).astype(jnp.bfloat16)
     flat_upgate = upgate_full.reshape(model_width, -1)
     paired = jnp.dot(normed_rows, flat_upgate, preferred_element_type=jnp.float32).reshape(
@@ -300,13 +321,9 @@
     grad_hidden = jnp.dot(cot_half, down_full.T, preferred_element_type=jnp.float32)
     grad_paired = swiglu_back(grad_hidden)[0].reshape(row_count, -1).astype(jnp.bfloat16)
     grad_normed_two = tensor_total(
-        jnp.dot(grad_paired, flat_upgate.T, preferred_element_type=jnp.float32).astype(
-            jnp.bfloat16
-        )
-    )
-    output_part = jnp.dot(hidden_half, down_full, preferred_element_type=jnp.float32).astype(
-        jnp.bfloat16
-    )
+        jnp.dot(grad_paired, flat_upgate.T, preferred_element_type=jnp.float32)
+    )
+    output_part = jnp.dot(hidden_half, down_full, preferred_element_type=jnp.float32)
     grad_down = jnp.dot(
         hidden_half.T, cot_half, preferred_element_type=jnp.float32
     ).astype(jnp.bfloat16)
@@ -315,10 +332,7 @@
         .astype(jnp.bfloat16)
         .reshape(upgate_full.shape)
     )
-    grad_normed_two, output_part, grad_down, grad_upgate = lax.optimization_barrier(
-        (grad_normed_two, output_part, grad_down, grad_upgate)
-    )
-    grad_normed_two = grad_normed_two.astype(jnp.float32)
+    grad_normed_two, output_part = lax.optimization_barrier((grad_normed_two, output_part))
     shard_upgate = lax.psum_scatter(grad_upgate, "dp", scatter_dimension=0, tiled=True)
     shard_down = lax.psum_scatter(grad_down, "dp", scatter_dimension=1, tiled=True)
     output_total = tensor_total(output_part)
@@ -352,17 +366,14 @@
     )
     partial_first = jnp.dot(
         joint_grad_half, joint_full.T, preferred_element_type=jnp.float32
-    ).astype(jnp.bfloat16)
-    partial_first, output_total, shard_upgate, shard_down, shard_out = lax.optimization_barrier(
-        (partial_first, output_total, shard_upgate, shard_down, shard_out)
-    )
-    output_rows = middle + output_total.astype(jnp.float32)
+    )
+    output_rows = middle + output_total
     shard_upgate, shard_down, shard_out = (
         shard_upgate.astype(jnp.float32),
         shard_down.astype(jnp.float32),
         shard_out.astype(jnp.float32),
     )
-    grad_normed_one = lax.psum(partial_first, "tensor").astype(jnp.float32)
+    grad_normed_one = tensor_total(partial_first)
     grad_joint = jnp.dot(normed_one.T, joint_grad_half, preferred_element_type=jnp.float32)
     shard_joint = lax.psum_scatter(
         grad_joint.astype(jnp.bfloat16), "dp", scatter_dimension=0, tiled=True
@@ -403,7 +414,7 @@
         ]
     )
     late = jnp.concatenate([grad_gain_one / tensor_count, grad_gain_part, local_squares])
-    late = gathered_total(late, ("tensor", "dp"))
+    late = gathered_total(tensor_total(late, False), "dp")
     grad_norm_gains = jnp.stack([late[:model_width], grad_gain_two])
     grad_out_gain = late[model_width : model_width + out_gain.size]
     total_squares = late[model_width + out_gain.size : model_width + out_gain.size + 8]

time: 609 us -> 387 us (0.64)
  waiting for transfers between devices: 319 us -> 107 us
  blocking collectives: 54.3 us -> 28.8 us
  starting transfers between devices: 0.88 us -> 21.5 us
  matrix products: 77.9 us -> 69.2 us
    psum x4 -> x0, waiting for transfers between devices: 153 us -> none  [the longest x3 132 us: tensor_total(): return lax.psum(partial_value, 'tensor')]
    ppermute x0 -> x18, waiting for transfers between devices: none -> 51.5 us  [the longest x16 49.3 us: exchange_total(): other = lax.ppermute(rounded.astype(jnp.bfloat16), 'tensor', pairs)]
    all_gather x1, waiting for transfers between devices: 37.8 us -> 0.01 us  [body(): lax.all_gather(upgate_weight.astype(jnp.bfloat16), 'dp', axis=0, tiled=True)]
    reduce_scatter x1, waiting for transfers between devices: 41.5 us -> 9.05 us  [body(): lax.psum_scatter(grad_joint.astype(jnp.bfloat16), 'dp', scatter_dimension...]
    unnamed x15 -> x11, waiting for transfers between devices: 30 us -> 0.14 us
    all_gather x2, blocking collectives: 54.3 us -> 28.8 us  [gathered_total(): blocks = lax.all_gather(block, axis_names, axis=0, tiled=True)]
    ppermute x0 -> x18, starting transfers between devices: none -> 21 us  [the longest x16 18 us: exchange_total(): other = lax.ppermute(rounded.astype(jnp.bfloat16), 'tensor', pairs)]
    all_gather x1, waiting for transfers between devices: 17.8 us -> 9.61 us  [body(): lax.all_gather(down_weight.astype(jnp.bfloat16), 'dp', axis=1, tiled=True)]
  transfers between devices with their start and end apart: 12 -> 26, of which waited for: 9 -> 18; matrix products, arithmetic and copies ran while one was open for 23% -> 40% of each run, Pallas kernels for 0% -> 0%
where the time goes in v2:
time: 387 us; the launch traced here: 382 us
  waiting for transfers between devices  107 us (28%)
  matrix products  69.2 us (18%)
  local copies, waits for them, and re-layouts  66.3 us (17%)
  other arithmetic  64 us (17%)
  blocking collectives  28.8 us (7%)
  between operations  25.7 us (7%)
  starting transfers between devices  21.5 us (6%)
    ppermute x16, waiting for transfers between devices, exchange_total(): other = lax.ppermute(rounded.astype(jnp.bfloat16), 'tensor', pairs)  49.3 us
    all_gather x1, waiting for transfers between devices, body(): joint_full = lax.all_gather(joint_shard, 'dp', axis=0, tiled=True)  36.4 us
    unnamed x355, local copies, waits for them, and re-layouts  29.7 us
    all_gather x2, blocking collectives, gathered_total(): blocks = lax.all_gather(block, axis_names, axis=0, tiled=True)  28.8 us
    ppermute x16, starting transfers between devices, exchange_total(): other = lax.ppermute(rounded.astype(jnp.bfloat16), 'tensor', pairs)  18 us
    sub x10, other arithmetic, adamw_update(): return (weight - rate * update, new_moment, new_second)  12.6 us
    reduce_sum x9, other arithmetic, square_sum(): return jnp.sum(values * values)  9.9 us
    all_gather x1, waiting for transfers between devices, body(): lax.all_gather(down_weight.astype(jnp.bfloat16), 'dp', axis=1, tiled=True)  9.61 us
  transfers between devices with their start and end apart: 26, of which 18 were waited for; matrix products, arithmetic and copies ran while one was open for 40% of the time, Pallas kernels for 0%

profile of v2, /device:TPU:0, one launch (start us, length us, event | category | flops | bytes accessed | tf_op | source)
XLA Modules:
  0.0 382.2 jit_solution(12628309284947974917)
XLA Ops:
  17.1 36.4 %all-gather.5.cloned.1.call-done = bf16[1024,1664]{1,0:T(8,128)(2,1)} async-done(((bf16[128,1664]{1,0:T(8,128)(2,1)}), bf16[1024,1664]{1,0:T(8,128)(2,1)}) %all-gather.5.cloned.1.call-update) | async-done | bytes 3407888 | tf_op jit(solution)/shard_map/all_gather | solution.py:284
  53.5 3.6 fusion.206
  59.3 4.1 %reshape.1084 = f32[1,384,2,768]{3,2,1,0:T(2,128)} reshape(f32[384,1536]{1,0:T(8,128)} %slice.302) | data formatting | bytes 4718592 | tf_op jit(solution)/shard_map/reshape | solution.py:295
  94.6 2.5 multiply_convert_fusion.3
  104.1 8.2 %collective-permute-done = bf16[192,1024]{1,0:T(8,128)(2,1)S(1)} collective-permute-done((bf16[192,1024]{1,0:T(8,128)(2,1)S(1)}, bf16[192,1024]{1,0:T(8,128)(2,1)S(1)}, u32[]{:S(2)}, u32[]{:S(2)}) %collective-permute-start) | collective-permute-done | bytes 393248 | tf_op jit(solution)/shard_map/ppermute | solution.py:213
  115.9 8.0 %collective-permute-done.1 = bf16[192,1024]{1,0:T(8,128)(2,1)S(1)} collective-permute-done((bf16[192,1024]{1,0:T(8,128)(2,1)S(1)}, bf16[192,1024]{1,0:T(8,128)(2,1)S(1)}, u32[]{:S(2)}, u32[]{:S(2)}) %collective-permute-start.1) | collective-permute-done | bytes 393248 | tf_op jit(solution)/shard_map/ppermute | solution.py:213
  128.1 5.4 %fusion = f32[384,2,704]{0,2,1:T(8,128)} fusion(bf16[1024,2,704]{0,2,1:T(8,128)(2,1)} %all-gather.9.cloned.1.call-done, f32[384,1024]{1,0:T(8,128)} %get-tuple-element.154, f32[1024]{0:T(1024)} %bitcast.580, f32[384]{0:T(512)} %fusion.188), kind=kOutput, calls=%fused_computation.2 | convolution fusion | flops 1108475904 | bytes 6624768 | tf_op jit(solution)/shard_map/dot_general | solution.py:315
  133.5 9.6 %all-gather.11.cloned.1.call-done = bf16[704,1024]{1,0:T(8,128)(2,1)} async-done(((bf16[704,128]{1,0:T(8,128)(2,1)}), bf16[704,1024]{1,0:T(8,128)(2,1)}) %all-gather.11.cloned.1.call-update) | async-done | bytes 1441808 | tf_op jit(solution)/shard_map/all_gather | solution.py:289
  143.2 3.7 multiply_bitcast_fusion
  152.1 9.6 %collective-permute-done.4 = bf16[192,1024]{1,0:T(8,128)(2,1)S(1)} collective-permute-done((bf16[192,1024]{1,0:T(8,128)(2,1)S(1)}, bf16[192,1024]{1,0:T(8,128)(2,1)S(1)}, u32[]{:S(2)}, u32[]{:S(2)}) %collective-permute-start.4) | collective-permute-done | bytes 393248 | tf_op jit(solution)/shard_map/ppermute | solution.py:213
  167.1 2.6 copy.276
  169.7 2.5 fusion.231
  178.8 6.5 %collective-permute-done.8 = bf16[192,1024]{1,0:T(8,128)(2,1)S(1)} collective-permute-done((bf16[192,1024]{1,0:T(8,128)(2,1)S(1)}, bf16[192,1024]{1,0:T(8,128)(2,1)S(1)}, u32[]{:S(2)}, u32[]{:S(2)}) %collective-permute-start.8) | collective-permute-done | bytes 393248 | tf_op jit(solution)/shard_map/ppermute | solution.py:213
  189.7 4.8 %collective-permute-done.9 = bf16[192,1024]{1,0:T(8,128)(2,1)S(1)} collective-permute-done((bf16[192,1024]{1,0:T(8,128)(2,1)S(1)}, bf16[192,1024]{1,0:T(8,128)(2,1)S(1)}, u32[]{:S(2)}, u32[]{:S(2)}) %collective-permute-start.9) | collective-permute-done | bytes 393248 | tf_op jit(solution)/shard_map/ppermute | solution.py:213
  200.7 3.6 copy.272
  204.3 2.4 copy.285
  206.8 5.2 %convolution_convert_fusion = bf16[1024,1408]{1,0:T(8,128)(2,1)} fusion(bf16[384,1408]{0,1:T(8,128)(2,1)} %bitcast.561, f32[384,1024]{1,0:T(8,128)} %get-tuple-element.154, f32[1024]{0:T(1024)} %bitcast.581, f32[384]{0:T(512)} %fusion.188), kind=kOutput, calls=%fused_computation | convolution fusion | flops 1109917696 | bytes 5543424 | tf_op jit(solution)/shard_map/dot_general | solution.py:331
  212.4 4.0 %multiply_reduce_fusion.11 = (f32[256]{0:T(256)}, f32[2,384]{1,0:T(2,128)S(1)}, f32[1,2,384,256]{3,2,1,0:T(8,128)S(1)}, f32[1,2,384,256]{3,2,1,0:T(8,128)S(1)}) fusion(f32[1,2,6,64,256]{4,3,2,1,0:T(8,128)} %get-tuple-element.235, f32[2,384]{1,0:T(2,128)} %copy-done.119, f32[1,2,384,768]{3,2,1,0:T(8,128)} %bitcast.550, f32[256]{0:T(256)} %param.40, ...), kind=kOutput, calls=%fused_computation.142 | convolution fusion | flops 406780928 | bytes 5775360 | tf_op jit(solution)/shard_map/dot_general | solution.py:350
  229.1 2.1 fusion.91
  247.3 5.2 %concatenate.40 = bf16[384,1664]{0,1:T(8,128)(2,1)S(1)} concatenate(bf16[384,1536]{0,1:T(8,128)(2,1)} %bitcast.565, bf16[384,4]{0,1:T(4,128)(2,1)S(1)} %reshape.1116, bf16[384,124]{0,1:T(8,128)(2,1)S(1)} %broadcast_in_dim.160), dimensions={1} | concatenate | bytes 2555904 | tf_op jit(solution)/shard_map/concatenate | solution.py:359
  252.6 4.0 %convolution_convert_fusion.1 = bf16[1024,1664]{1,0:T(8,128)(2,1)} fusion(bf16[384,1664]{0,1:T(8,128)(2,1)S(1)} %concatenate.40, f32[384,1024]{1,0:T(8,128)S(1)} %copy-done, f32[1024]{0:T(1024)S(1)} %bitcast.589, f32[384]{0:T(512)S(1)} %copy-done.122), kind=kOutput, calls=%fused_computation.1 | convolution fusion | flops 1311506432 | bytes 6264320 | tf_op jit(solution)/shard_map/dot_general | solution.py:377
  257.3 4.0 %fusion.232 = f32[384,1024]{1,0:T(8,128)S(1)} fusion(bf16[384,1664]{0,1:T(8,128)(2,1)} %copy-done.57, bf16[1024,1664]{1,0:T(8,128)(2,1)} %all-gather.5.cloned.1.call-done), kind=kOutput, calls=%fused_computation.458 | convolution fusion | flops 1308622848 | bytes 6258688 | tf_op jit(solution)/shard_map/dot_general | solution.py:367
  269.5 14.9 %all_gather.22 = f32[64,768]{1,0:T(8,128)S(1)} all-gather(f32[8,768]{1,0:T(8,128)} %reshape.1120), channel_id=1, replica_groups=mesh['tensor'=4,'dp'=8] {'dp'}, dimensions={0}, use_global_device_ids=true | all-gather | bytes 221184 | tf_op jit(solution)/shard_map/all_gather | solution.py:203
  287.7 2.1 fusion.83
  297.0 4.6 %collective-permute-done.13 = bf16[192,1024]{1,0:T(8,128)(2,1)} collective-permute-done((bf16[192,1024]{1,0:T(8,128)(2,1)}, bf16[192,1024]{1,0:T(8,128)(2,1)}, u32[]{:S(2)}, u32[]{:S(2)}) %collective-permute-start.13) | collective-permute-done | bytes 393248 | tf_op jit(solution)/shard_map/ppermute | solution.py:213
  311.4 2.7 multiply_reduce_fusion.15
  314.0 9.1 %reduce-scatter.11.cloned.1.call-done = bf16[128,1664]{1,0:T(8,128)(2,1)} async-done(((bf16[1024,1664]{1,0:T(8,128)(2,1)}), bf16[128,1664]{1,0:T(8,128)(2,1)}) %reduce-scatter.11.cloned.1.call-update) | async-done | bytes 426000 | tf_op jit(solution)/shard_map/reduce_scatter | solution.py:378
  325.6 3.3 concatenate.43
  330.4 2.2 collective-permute-done.16
  334.1 2.9 fusion.9
  339.2 14.0 %all_gather.23 = f32[64,256]{1,0:T(8,128)S(1)} all-gather(f32[8,256]{1,0:T(8,128)S(1)} %reshape.1123), channel_id=1, replica_groups=mesh['tensor'=4,'dp'=8] {'dp'}, dimensions={0}, use_global_device_ids=true | all-gather | bytes 73728 | tf_op jit(solution)/shard_map/all_gather | solution.py:203
  363.5 5.1 %multiply_subtract_fusion = (f32[128,2,768]{2,1,0:T(2,128)}, f32[128,2,768]{2,1,0:T(2,128)}, f32[128,2,768]{2,1,0:T(2,128)}) fusion(f32[128,2,768]{2,1,0:T(2,128)S(1)} %copy-done.41, f32[128,2,768]{2,1,0:T(2,128)S(1)} %reshape.1125, f32[]{:T(128)} %bitcast.147, f32[128,2,768]{2,1,0:T(2,128)} %param.45, f32[128,2,768]{2,1,0:T(2,128)} %param.55), kind=kLoop, calls=%fused_computation.139 | loop fusion | flops 3145728 | bytes 5505028 | tf_op jit(solution)/shard_map/sub | solution.py:193
  (581 shorter events, 157.8 us)
Async XLA Ops:
  7.3 46.2 %all-gather.5.cloned.1.call-start = ((), (), s32[]{:S(2)}) async-start(), calls=%async_computation.4 | async-start | bytes 3833856 | tf_op jit(solution)/shard_map/all_gather | solution.py:284
  9.9 89.1 %all-gather.7.cloned.1.call-start = ((), (), s32[]{:S(2)}) async-start(), calls=%async_computation.5 | async-start | bytes 1179648 | tf_op jit(solution)/shard_map/all_gather | solution.py:285
  10.6 117.5 %all-gather.9.cloned.1.call-start = ((), (), s32[]{:S(2)}) async-start(), calls=%async_computation.6 | async-start | bytes 3244032 | tf_op jit(solution)/shard_map/all_gather | solution.py:286
  11.5 131.6 %all-gather.11.cloned.1.call-start = ((), (), s32[]{:S(2)}) async-start(), calls=%async_computation.7 | async-start | bytes 1622016 | tf_op jit(solution)/shard_map/all_gather | solution.py:289
  12.3 292.8 %reduce-scatter.17.cloned.1.call-start = ((), (), s32[]{:S(2)}) async-start(), calls=%async_computation.11 | async-start | bytes 1769472
  15.7 50.9 %copy-start.93 = (f32[2,512]{1,0:T(2,128)}, f32[2,512]{1,0:T(2,128)S(1)}, u32[]{:S(2)}) copy-start(f32[2,512]{1,0:T(2,128)S(1)} %get-tuple-element.205) | copy-start | bytes 12292
  15.8 50.9 %copy-start.95 = (f32[2,512]{1,0:T(2,128)}, f32[2,512]{1,0:T(2,128)S(1)}, u32[]{:S(2)}) copy-start(f32[2,512]{1,0:T(2,128)S(1)} %get-tuple-element.206) | copy-start | bytes 12292
  15.8 50.8 %copy-start.97 = (f32[2,512]{1,0:T(2,128)}, f32[2,512]{1,0:T(2,128)S(1)}, u32[]{:S(2)}) copy-start(f32[2,512]{1,0:T(2,128)S(1)} %get-tuple-element.207) | copy-start | bytes 12292
  15.8 56.3 %copy-start.155 = (f32[2]{0:T(128)}, f32[2]{0:T(128)S(1)}, u32[]{:S(2)}) copy-start(f32[2]{0:T(128)S(1)} %exponential_negate_fusion) | copy-start | bytes 28
  101.1 11.2 %collective-permute-start = (bf16[192,1024]{1,0:T(8,128)(2,1)S(1)}, bf16[192,1024]{1,0:T(8,128)(2,1)S(1)}, u32[]{:S(2)}, u32[]{:S(2)}) collective-permute-start(bf16[192,1024]{1,0:T(8,128)(2,1)S(1)} %get-tuple-element.191), channel_id=1, source_target_pairs={{0,8},{8,0},{16,24},{24,16},{1,9},{9,1},{17,25},{25,17},{2,10},{10... | collective-permute-start | bytes 1179656 | tf_op jit(solution)/shard_map/ppermute | solution.py:213
  102.7 10.8 %collective-permute-start.2 = (bf16[192,1024]{1,0:T(8,128)(2,1)S(1)}, bf16[192,1024]{1,0:T(8,128)(2,1)S(1)}, u32[]{:S(2)}, u32[]{:S(2)}) collective-permute-start(bf16[192,1024]{1,0:T(8,128)(2,1)S(1)} %get-tuple-element.192), channel_id=1, source_target_pairs={{0,16},{8,24},{16,0},{24,8},{1,17},{9,25},{17,1},{25,9},{2,18},{10... | collective-permute-start | bytes 1179656 | tf_op jit(solution)/shard_map/ppermute | solution.py:213
  113.8 10.1 %collective-permute-start.1 = (bf16[192,1024]{1,0:T(8,128)(2,1)S(1)}, bf16[192,1024]{1,0:T(8,128)(2,1)S(1)}, u32[]{:S(2)}, u32[]{:S(2)}) collective-permute-start(bf16[192,1024]{1,0:T(8,128)(2,1)S(1)} %get-tuple-element.189), channel_id=1, source_target_pairs={{0,16},{8,24},{16,0},{24,8},{1,17},{9,25},{17,1},{25,9},{2,18},{10... | collective-permute-start | bytes 1179656 | tf_op jit(solution)/shard_map/ppermute | solution.py:213
  115.3 9.8 %collective-permute-start.3 = (bf16[192,1024]{1,0:T(8,128)(2,1)S(1)}, bf16[192,1024]{1,0:T(8,128)(2,1)S(1)}, u32[]{:S(2)}, u32[]{:S(2)}) collective-permute-start(bf16[192,1024]{1,0:T(8,128)(2,1)S(1)} %get-tuple-element.190), channel_id=1, source_target_pairs={{0,8},{8,0},{16,24},{24,16},{1,9},{9,1},{17,25},{25,17},{2,10},{10... | collective-permute-start | bytes 1179656 | tf_op jit(solution)/shard_map/ppermute | solution.py:213
  150.4 11.3 %collective-permute-start.4 = (bf16[192,1024]{1,0:T(8,128)(2,1)S(1)}, bf16[192,1024]{1,0:T(8,128)(2,1)S(1)}, u32[]{:S(2)}, u32[]{:S(2)}) collective-permute-start(bf16[192,1024]{1,0:T(8,128)(2,1)S(1)} %get-tuple-element.185), channel_id=1, source_target_pairs={{0,8},{8,0},{16,24},{24,16},{1,9},{9,1},{17,25},{25,17},{2,10},{10... | collective-permute-start | bytes 1179656 | tf_op jit(solution)/shard_map/ppermute | solution.py:213
  150.7 11.2 %collective-permute-start.6 = (bf16[192,1024]{1,0:T(8,128)(2,1)S(1)}, bf16[192,1024]{1,0:T(8,128)(2,1)S(1)}, u32[]{:S(2)}, u32[]{:S(2)}) collective-permute-start(bf16[192,1024]{1,0:T(8,128)(2,1)S(1)} %get-tuple-element.186), channel_id=1, source_target_pairs={{0,16},{8,24},{16,0},{24,8},{1,17},{9,25},{17,1},{25,9},{2,18},{10... | collective-permute-start | bytes 1179656 | tf_op jit(solution)/shard_map/ppermute | solution.py:213
  163.0 10.8 %collective-permute-start.5 = (bf16[192,1024]{1,0:T(8,128)(2,1)}, bf16[192,1024]{1,0:T(8,128)(2,1)}, u32[]{:S(2)}, u32[]{:S(2)}) collective-permute-start(bf16[192,1024]{1,0:T(8,128)(2,1)} %get-tuple-element.183), channel_id=1, source_target_pairs={{0,16},{8,24},{16,0},{24,8},{1,17},{9,25},{17,1},{25,9},{2,18},{10... | collective-permute-start | bytes 1179656 | tf_op jit(solution)/shard_map/ppermute | solution.py:213
  164.3 10.2 %collective-permute-start.7 = (bf16[192,1024]{1,0:T(8,128)(2,1)}, bf16[192,1024]{1,0:T(8,128)(2,1)}, u32[]{:S(2)}, u32[]{:S(2)}) collective-permute-start(bf16[192,1024]{1,0:T(8,128)(2,1)} %get-tuple-element.184), channel_id=1, source_target_pairs={{0,8},{8,0},{16,24},{24,16},{1,9},{9,1},{17,25},{25,17},{2,10},{10... | collective-permute-start | bytes 1179656 | tf_op jit(solution)/shard_map/ppermute | solution.py:213
  169.6 137.3 %reduce-scatter.13.cloned.1.call-start = ((), (), s32[]{:S(2)}) async-start(), calls=%async_computation.9 | async-start | bytes 1179648
  176.3 9.0 %collective-permute-start.8 = (bf16[192,1024]{1,0:T(8,128)(2,1)S(1)}, bf16[192,1024]{1,0:T(8,128)(2,1)S(1)}, u32[]{:S(2)}, u32[]{:S(2)}) collective-permute-start(bf16[192,1024]{1,0:T(8,128)(2,1)S(1)} %get-tuple-element.179), channel_id=1, source_target_pairs={{0,8},{8,0},{16,24},{24,16},{1,9},{9,1},{17,25},{25,17},{2,10},{10... | collective-permute-start | bytes 1179656 | tf_op jit(solution)/shard_map/ppermute | solution.py:213
  177.2 8.8 %collective-permute-start.10 = (bf16[192,1024]{1,0:T(8,128)(2,1)S(1)}, bf16[192,1024]{1,0:T(8,128)(2,1)S(1)}, u32[]{:S(2)}, u32[]{:S(2)}) collective-permute-start(bf16[192,1024]{1,0:T(8,128)(2,1)S(1)} %get-tuple-element.180), channel_id=1, source_target_pairs={{0,16},{8,24},{16,0},{24,8},{1,17},{9,25},{17,1},{25,9},{2,18},{10... | collective-permute-start | bytes 1179656 | tf_op jit(solution)/shard_map/ppermute | solution.py:213
  186.3 8.1 %collective-permute-start.9 = (bf16[192,1024]{1,0:T(8,128)(2,1)S(1)}, bf16[192,1024]{1,0:T(8,128)(2,1)S(1)}, u32[]{:S(2)}, u32[]{:S(2)}) collective-permute-start(bf16[192,1024]{1,0:T(8,128)(2,1)S(1)} %get-tuple-element.177), channel_id=1, source_target_pairs={{0,16},{8,24},{16,0},{24,8},{1,17},{9,25},{17,1},{25,9},{2,18},{10... | collective-permute-start | bytes 1179656 | tf_op jit(solution)/shard_map/ppermute | solution.py:213
  188.0 7.8 %collective-permute-start.11 = (bf16[192,1024]{1,0:T(8,128)(2,1)S(1)}, bf16[192,1024]{1,0:T(8,128)(2,1)S(1)}, u32[]{:S(2)}, u32[]{:S(2)}) collective-permute-start(bf16[192,1024]{1,0:T(8,128)(2,1)S(1)} %get-tuple-element.178), channel_id=1, source_target_pairs={{0,8},{8,0},{16,24},{24,16},{1,9},{9,1},{17,25},{25,17},{2,10},{10... | collective-permute-start | bytes 1179656 | tf_op jit(solution)/shard_map/ppermute | solution.py:213
  206.8 102.7 %reduce-scatter.15.cloned.1.call-start = ((), (), s32[]{:S(2)}) async-start(), calls=%async_computation.10 | async-start | bytes 3244032
  212.1 111.0 %reduce-scatter.11.cloned.1.call-start = ((), (), s32[]{:S(2)}) async-start(), calls=%async_computation.8 | async-start | bytes 3833856 | tf_op jit(solution)/shard_map/reduce_scatter | solution.py:378
  262.4 25.3 %collective-permute-start.12 = (bf16[192,1024]{1,0:T(8,128)(2,1)}, bf16[192,1024]{1,0:T(8,128)(2,1)S(1)}, u32[]{:S(2)}, u32[]{:S(2)}) collective-permute-start(bf16[192,1024]{1,0:T(8,128)(2,1)} %get-tuple-element.165), channel_id=1, source_target_pairs={{0,8},{8,0},{16,24},{24,16},{1,9},{9,1},{17,25},{25,17},{2,10},{10... | collective-permute-start | bytes 1179656 | tf_op jit(solution)/shard_map/ppermute | solution.py:213
  263.3 24.4 %collective-permute-start.14 = (bf16[192,1024]{1,0:T(8,128)(2,1)}, bf16[192,1024]{1,0:T(8,128)(2,1)}, u32[]{:S(2)}, u32[]{:S(2)}) collective-permute-start(bf16[192,1024]{1,0:T(8,128)(2,1)} %get-tuple-element.166), channel_id=1, source_target_pairs={{0,16},{8,24},{16,0},{24,8},{1,17},{9,25},{17,1},{25,9},{2,18},{10... | collective-permute-start | bytes 1179656 | tf_op jit(solution)/shard_map/ppermute | solution.py:213
  289.9 11.7 %collective-permute-start.13 = (bf16[192,1024]{1,0:T(8,128)(2,1)}, bf16[192,1024]{1,0:T(8,128)(2,1)}, u32[]{:S(2)}, u32[]{:S(2)}) collective-permute-start(bf16[192,1024]{1,0:T(8,128)(2,1)} %get-tuple-element.163), channel_id=1, source_target_pairs={{0,16},{8,24},{16,0},{24,8},{1,17},{9,25},{17,1},{25,9},{2,18},{10... | collective-permute-start | bytes 1179656 | tf_op jit(solution)/shard_map/ppermute | solution.py:213
  290.9 11.4 %collective-permute-start.15 = (bf16[192,1024]{1,0:T(8,128)(2,1)}, bf16[192,1024]{1,0:T(8,128)(2,1)}, u32[]{:S(2)}, u32[]{:S(2)}) collective-permute-start(bf16[192,1024]{1,0:T(8,128)(2,1)} %get-tuple-element.164), channel_id=1, source_target_pairs={{0,8},{8,0},{16,24},{24,16},{1,9},{9,1},{17,25},{25,17},{2,10},{10... | collective-permute-start | bytes 1179656 | tf_op jit(solution)/shard_map/ppermute | solution.py:213
  293.1 76.2 %copy-start.84 = (f32[4,2,512]{2,1,0:T(2,128)}, f32[4,2,512]{2,1,0:T(2,128)S(1)}, u32[]{:S(2)}) copy-start(f32[4,2,512]{2,1,0:T(2,128)S(1)} %get-tuple-element.145) | copy-start | bytes 49156
  306.9 67.0 %copy-start.56 = (f32[704,128]{1,0:T(8,128)}, f32[704,128]{1,0:T(8,128)S(1)}, u32[]{:S(2)}) copy-start(f32[704,128]{1,0:T(8,128)S(1)} %get-tuple-element.147) | copy-start | bytes 1081348
  328.9 3.7 collective-permute-start.16
  332.6 5.9 %collective-permute-start.17 = (f32[1288]{0:T(1024)S(1)}, f32[1288]{0:T(1024)}, u32[]{:S(2)}, u32[]{:S(2)}) collective-permute-start(f32[1288]{0:T(1024)S(1)} %add.587), channel_id=1, source_target_pairs={{0,16},{8,24},{16,0},{24,8},{1,17},{9,25},{17,1},{25,9},{2,18},{10... | collective-permute-start | bytes 15464 | tf_op jit(solution)/shard_map/ppermute | solution.py:216
  (166 other events, 1065.2 us)
Sparse Core Ops, SparseCore 0:
  10.3 43.1 all-gather.4
  55.6 22.8 all-gather.6
  80.7 35.6 all-gather.8
  118.3 24.7 all-gather.10
  169.8 34.1 reduce-scatter.16
  206.9 32.0 reduce-scatter.12
  241.4 37.4 reduce-scatter.14
  281.1 41.9 reduce-scatter.10
